TPU v7x, 128 devices: a whole 4x4x4 slice. The times are simulated.
128 devices in a mesh: gx: 8 (over y, core), gy: 16 (over x, z).
Axes of the slice: x: 4, y: 4, z: 4, core: 2. Of those that a mesh axis runs over, the one named last changes fastest.
Arguments:
- control: float32 [3, 512, 2048], P(None, 'gy', 'gx'), may hold values from -2 to 2
- perts: float32 [16, 3, 512, 2048], P(None, None, 'gy', 'gx'), may hold values from -2.8 to 2.8
Outputs:
- basis: float32 [16, 3, 512, 2048], P(None, None, 'gy', 'gx')
- rfactor: float32 [16, 16], replicated
All inputs are finite; a program needn't handle non-finite values.
Results may differ from a plain program's by a relative error of at most 0.0003.
Values sent between devices are 32-bit elements; how exact they have to be, the bound alone decides.
A program may use at most 64 MiB of HBM per device.

v0:
```python
import functools
import math

import jax
import jax.numpy as jnp
from jax import lax
from jax.experimental import pallas as pl
from jax.experimental.pallas import tpu as pltpu
from jax.sharding import PartitionSpec as P

MESH = pl.DeviceIdType.MESH
HALO = 8
STEPS = 2
MEAN_DEPTH = 4.0
TIME_STEP = 0.1
HIGHEST = lax.Precision.HIGHEST


def slope(minus2, minus1, plus1, plus2):
    return (plus1 - minus1) - 0.125 * (plus2 - minus2)


def kernel(
    nx_dev, ny_dev, members, rows, cols,
    ctrl_hbm, perts_hbm, basis_ref, rfac_ref,
    st, pk, halo, nat, now, mid, cini, cfin, cor, fin, red1, red2,
    in_sem, y_send, y_recv, x_send, x_recv, r1_send, r1_recv, r2_send, r2_recv,
):
    gx, gy = lax.axis_index("gx"), lax.axis_index("gy")
    ext = rows + 2 * HALO
    tall = ext // 8
    states = members + 1
    lane = lax.broadcasted_iota(jnp.int32, (8, 128), 1)
    sub = lax.broadcasted_iota(jnp.int32, (8, 128), 0)
    left, right = lax.rem(gx + nx_dev - 1, nx_dev), lax.rem(gx + 1, nx_dev)
    up, down = lax.rem(gy + ny_dev - 1, ny_dev), lax.rem(gy + 1, ny_dev)

    def own_copy(k):
        source = ctrl_hbm if k == 0 else perts_hbm.at[pl.ds((k - 1) * 4, 4)]
        target = st.at[0] if k == 0 else st.at[pl.ds((k - 1) * 4 + 1, 4)]
        if k == 0:
            return pltpu.make_async_copy(source, target.at[:, pl.ds(HALO, rows), :], in_sem.at[k])
        return pltpu.make_async_copy(source, target.at[:, :, pl.ds(HALO, rows), :], in_sem.at[k])

    for k in range(members // 4 + 1):
        own_copy(k).start()

    barrier = pltpu.get_barrier_semaphore()
    greeted = []
    for d in range(1, nx_dev):
        greeted.append((lax.rem(gx + d, nx_dev), gy))
    for d in range(1, ny_dev):
        greeted.append((gx, lax.rem(gy + d, ny_dev)))
    for a in (left, right):
        for b in (up, down):
            greeted.append((a, b))
    for peer in greeted:
        pl.semaphore_signal(barrier, inc=1, device_id=peer, device_id_type=MESH)

    grid_rows = rows * ny_dev
    for t in range(tall):
        row = lax.rem(gy * rows - HALO + tall * sub + t + grid_rows, grid_rows).astype(jnp.float32)
        cor[t] = 0.5 * (1.0 + 0.5 * jnp.sin(2.0 * math.pi * row / float(grid_rows)))
    cini[...] = jnp.zeros_like(cini)
    cfin[...] = jnp.zeros_like(cfin)

    pl.semaphore_wait(barrier, len(greeted))

    def y_copies(k, field_ref):
        return (
            pltpu.make_async_remote_copy(
                field_ref.at[:, pl.ds(0, HALO), :],
                st.at[k, :, pl.ds(HALO + rows, HALO), :],
                y_send.at[0, k], y_recv.at[0, k], device_id=(gx, up), device_id_type=MESH),
            pltpu.make_async_remote_copy(
                field_ref.at[:, pl.ds(rows - HALO, HALO), :],
                st.at[k, :, pl.ds(0, HALO), :],
                y_send.at[1, k], y_recv.at[1, k], device_id=(gx, down), device_id_type=MESH),
        )

    for copy in y_copies(0, ctrl_hbm):
        copy.start()

    @pl.loop(0, members)
    def _(m):
        for copy in y_copies(m + 1, perts_hbm.at[m]):
            copy.start()

    for k in range(members // 4 + 1):
        own_copy(k).wait()

    wide = lax.broadcasted_iota(jnp.int32, (rows, 128), 1) // 8

    @pl.loop(0, 3)
    def _(f):
        first = jnp.zeros((rows, 128), jnp.float32)
        last = jnp.zeros((rows, 128), jnp.float32)
        for m in range(members):
            head = st[m + 1, f, HALO : HALO + rows, 0:128]
            tail = st[m + 1, f, HALO : HALO + rows, cols - 128 : cols]
            first = jnp.where(wide == m, pltpu.roll(head, (8 * m) % 128, 1), first)
            last = jnp.where(wide == m, pltpu.roll(tail, (8 * m + 8) % 128, 1), last)
        pk[0, 0, f] = first
        pk[1, 0, f] = last
        pk[0, 1, f] = st[0, f, HALO : HALO + rows, 0:128]
        pk[1, 1, f] = pltpu.roll(st[0, f, HALO : HALO + rows, cols - 128 : cols], 8, 1)

    def x_copies():
        out = []
        for side, x_to in ((0, left), (1, right)):
            for place, (start, count, to, y_to) in enumerate(
                ((0, rows, HALO, gy), (0, HALO, HALO + rows, up), (rows - HALO, HALO, 0, down))
            ):
                out.append(
                    pltpu.make_async_remote_copy(
                        pk.at[side, :, :, pl.ds(start, count), :],
                        halo.at[side, :, :, pl.ds(to, count), :],
                        x_send.at[side, place], x_recv.at[side, place],
                        device_id=(x_to, y_to), device_id_type=MESH)
                )
        return out

    sent = x_copies()
    for copy in sent:
        copy.start()
    for copy in sent:
        copy.wait()

    def shifted(planes, d):
        turned = [pltpu.roll(p, (-d) % 128, 1) for p in planes]
        n = len(planes)
        if d > 0:
            return [jnp.where(lane < 128 - d, turned[i], turned[(i + 1) % n]) for i in range(n)]
        return [jnp.where(lane >= -d, turned[i], turned[(i - 1) % n]) for i in range(n)]

    def slope_x(planes):
        return [slope(*z) for z in zip(shifted(planes, -2), shifted(planes, -1), shifted(planes, 1), shifted(planes, 2))]

    def put(ref, f, t, i, value):
        ref[f, t + 2, i] = value
        if t < 2:
            ref[f, t + 2 + tall, i] = pltpu.roll(value, 7, 0)
        if t >= tall - 2:
            ref[f, t + 2 - tall, i] = pltpu.roll(value, 1, 0)

    def put_state(ref, t, i, h, e, n):
        put(ref, 0, t, i, h)
        put(ref, 1, t, i, e)
        put(ref, 2, t, i, n)
        put(ref, 3, t, i, (MEAN_DEPTH + h) * n)

    def changes(ref, t):
        h = [ref[0, t + 2, i] for i in range(3)]
        e = [ref[1, t + 2, i] for i in range(3)]
        n = [ref[2, t + 2, i] for i in range(3)]
        de = [(MEAN_DEPTH + a) * b for a, b in zip(h, e)]
        hx, ex, nx, dex = slope_x(h), slope_x(e), slope_x(n), slope_x(de)
        c = cor[t]
        out = []
        for i in range(3):
            hy, ey, ny, dny = (slope(ref[f, t, i], ref[f, t + 1, i], ref[f, t + 3, i], ref[f, t + 4, i]) for f in range(4))
            out.append((
                h[i], e[i], n[i],
                dex[i] + dny,
                e[i] * ex[i] + n[i] * ey + hx[i],
                e[i] * nx[i] + n[i] * ny + hy,
                c * n[i], c * e[i],
            ))
        return out

    full, half = TIME_STEP * (2.0 / 3.0), 0.5 * TIME_STEP * (2.0 / 3.0)

    @pl.loop(0, states)
    def _(k):
        m = jnp.maximum(k - 1, 0)
        tile = jnp.where(k == 0, 1, 0)
        for copy in y_copies(k, ctrl_hbm):
            copy.wait_recv()
        to_right = lax.rem(128 - 8 * m, 128)
        to_left = lax.rem(128 + 120 - 8 * m, 128)
        for f in range(3):
            for i in range(2):
                nat[f, i] = st[k, f, :, 128 * i : 128 * (i + 1)]
        for t in range(tall):
            pick = pl.ds(t, 8, stride=tall)
            planes = []
            for f in range(3):
                after = pltpu.roll(halo[0, tile, f, pick, :], to_right, 1)
                before = pltpu.roll(halo[1, tile, f, pick, :], to_left, 1)
                planes.append((
                    cini[f, t, 0] + nat[f, 0, pick, :],
                    cini[f, t, 1] + nat[f, 1, pick, :],
                    cini[f, t, 2] + jnp.where(lane < 64, after, before),
                ))
            for i in range(3):
                put_state(now, t, i, planes[0][i], planes[1][i], planes[2][i])

        @pl.when(k == 0)
        def _():
            for f in range(3):
                cini[f] = now[f, 2 : 2 + tall]

        @pl.loop(0, STEPS)
        def _(step):
            for t in range(tall):
                for i, (h, e, n, th, te, tn, cn, ce) in enumerate(changes(now, t)):
                    put_state(mid, t, i, h - full * th, e - full * te + TIME_STEP * cn, n - full * tn - TIME_STEP * ce)
            for t in range(tall):
                for i, (h, e, n, th, te, tn, cn, ce) in enumerate(changes(mid, t)):
                    put_state(
                        now, t, i,
                        0.5 * (now[0, t + 2, i] + h) - half * th,
                        0.5 * (now[1, t + 2, i] + e) - half * te + (0.5 * TIME_STEP) * cn,
                        0.5 * (now[2, t + 2, i] + n) - half * tn - (0.5 * TIME_STEP) * ce,
                    )

        for f in range(3):
            for t in range(tall):
                for i in range(2):
                    fin[k, f, i, pl.ds(t, 8, stride=tall), :] = now[f, t + 2, i] - cfin[f, t, i]

        @pl.when(k == 0)
        def _():
            for f in range(3):
                for i in range(2):
                    cfin[f, :, i] = now[f, 2 : 2 + tall, i]

    @pl.loop(0, states)
    def _(k):
        for copy in y_copies(k, ctrl_hbm):
            copy.wait_send()

    block = 8 * members

    def piece(f, r):
        both = [fin[1:, f, i, pl.ds(pl.multiple_of(HALO + 8 * r, 8), 8), :].reshape(block, 128) for i in range(2)]
        return jnp.concatenate(both, axis=1)

    def add_piece(j, total):
        x = piece(j // (rows // 8), lax.rem(j, rows // 8))
        return total + lax.dot_general(x, x, (((1,), (1,)), ((), ())), precision=HIGHEST, preferred_element_type=jnp.float32)

    pieces = 3 * rows // 8
    total = lax.fori_loop(0, pieces, add_piece, jnp.zeros((block, block), jnp.float32))
    r_id = lax.broadcasted_iota(jnp.int32, (block, block), 0)
    c_id = lax.broadcasted_iota(jnp.int32, (block, block), 1)
    same = lax.rem(r_id, 8) == lax.rem(c_id, 8)
    total = jnp.where(same, total, 0.0)
    total = jnp.sum(total.reshape(members, 8, block), axis=1)
    g_id = lax.broadcasted_iota(jnp.int32, (block, 128), 0) // 8
    l_id = lax.broadcasted_iota(jnp.int32, (block, 128), 1)
    gather = jnp.where(g_id == l_id, 1.0, 0.0)
    gram = jnp.dot(total, gather, precision=HIGHEST, preferred_element_type=jnp.float32)

    def all_sum(value, buf, me, count, peer_of, send, recv):
        buf[me] = value
        copies = []
        for d in range(1, count):
            copies.append(
                pltpu.make_async_remote_copy(
                    buf.at[me], buf.at[me], send.at[d], recv.at[d],
                    device_id=peer_of(lax.rem(me + d, count)), device_id_type=MESH)
            )
        for copy in copies:
            copy.start()
        for copy in copies:
            copy.wait_recv()
        out = buf[0]
        for d in range(1, count):
            out = out + buf[d]
        return out, copies

    packed = jnp.where(lane < members, gram[0:8], pltpu.roll(gram[8:16], members, 1))
    packed, sent1 = all_sum(packed, red1, gx, nx_dev, lambda i: (i, gy), r1_send, r1_recv)
    packed, sent2 = all_sum(packed, red2, gy, ny_dev, lambda i: (gx, i), r2_send, r2_recv)
    for copy in sent1 + sent2:
        copy.wait_send()
    gram = jnp.concatenate([packed, pltpu.roll(packed, 128 - members, 1)], axis=0)

    row_id = lax.broadcasted_iota(jnp.int32, (members, 128), 0)
    col_id = lax.broadcasted_iota(jnp.int32, (members, 128), 1)
    work = jnp.where(col_id < members, gram, jnp.where(col_id - members == row_id, 1.0, 0.0))
    for k in range(members):
        column = jnp.sum(jnp.where(col_id == k, work, 0.0), axis=1, keepdims=True)
        pivot = jnp.sqrt(column[k : k + 1])
        row = work[k : k + 1] / pivot
        factor = column / pivot
        work = jnp.where(row_id > k, work - factor * row, jnp.where(row_id == k, row, work))
    length = float(3 * grid_rows * cols * nx_dev)
    rfac_ref[...] = jnp.where(row_id <= col_id, work * (1.0 / math.sqrt(length)), 0.0)[:, :members]

    inverse = pltpu.roll(work, 128 - members, 1) * math.sqrt(length)
    s_id = lax.broadcasted_iota(jnp.int32, (128, block), 0)
    e_id = lax.broadcasted_iota(jnp.int32, (128, block), 1) // 8
    spread = jnp.where(s_id == e_id, 1.0, 0.0)
    big = jnp.dot(inverse, spread, precision=HIGHEST, preferred_element_type=jnp.float32)
    big = jnp.broadcast_to(big[:, None, :], (members, 8, block)).reshape(block, block)
    big = jnp.where(same & (r_id // 8 >= c_id // 8), big, 0.0)

    @pl.loop(0, pieces)
    def _(j):
        f, r = j // (rows // 8), lax.rem(j, rows // 8)
        y = jnp.dot(big, piece(f, r), precision=HIGHEST, preferred_element_type=jnp.float32)
        basis_ref[:, f, pl.ds(pl.multiple_of(8 * r, 8), 8), :] = y.reshape(members, 8, cols)


def body(control, perts):
    nx_dev, ny_dev = lax.axis_size("gx"), lax.axis_size("gy")
    members, _, rows, cols = perts.shape
    states, ext = members + 1, rows + 2 * HALO
    tall = ext // 8
    f32 = jnp.float32
    dma = pltpu.SemaphoreType.DMA
    return pl.pallas_call(
        functools.partial(kernel, nx_dev, ny_dev, members, rows, cols),
        out_shape=(
            jax.ShapeDtypeStruct(perts.shape, f32),
            jax.ShapeDtypeStruct((members, members), f32),
        ),
        in_specs=[pl.BlockSpec(memory_space=pl.ANY)] * 2,
        out_specs=[pl.BlockSpec(memory_space=pltpu.VMEM)] * 2,
        scratch_shapes=[
            pltpu.VMEM((states, 3, ext, cols), f32),
            pltpu.VMEM((2, 2, 3, rows, 128), f32),
            pltpu.VMEM((2, 2, 3, ext, 128), f32),
            pltpu.VMEM((3, 2, ext, 128), f32),
            pltpu.VMEM((4, tall + 4, 3, 8, 128), f32),
            pltpu.VMEM((4, tall + 4, 3, 8, 128), f32),
            pltpu.VMEM((3, tall, 3, 8, 128), f32),
            pltpu.VMEM((3, tall, 2, 8, 128), f32),
            pltpu.VMEM((tall, 8, 128), f32),
            pltpu.VMEM((states, 3, 2, ext, 128), f32),
            pltpu.VMEM((nx_dev, 8, 128), f32),
            pltpu.VMEM((ny_dev, 8, 128), f32),
            dma((members // 4 + 1,)),
            dma((2, states)),
            dma((2, states)),
            dma((2, 3)),
            dma((2, 3)),
            dma((nx_dev,)),
            dma((nx_dev,)),
            dma((ny_dev,)),
            dma((ny_dev,)),
        ],
        compiler_params=pltpu.CompilerParams(
            collective_id=0, has_side_effects=True, vmem_limit_bytes=40 * 1024 * 1024
        ),
    )(control, perts)


def solution(mesh):
    in_specs = (P(None, "gy", "gx"), P(None, None, "gy", "gx"))
    out_specs = (P(None, None, "gy", "gx"), P())
    return jax.shard_map(body, mesh=mesh, in_specs=in_specs, out_specs=out_specs, check_vma=False)
```

profile of v0, /device:TPU:1, one launch (start us, length us, event | category | flops | bytes accessed | tf_op | source)
XLA Modules:
  0.0 72.2 jit_solution(12736518878498772551)
XLA Ops:
  0.6 0.0 copy-start
  0.6 1.4 %copy-done = f32[16,3,32,256]{3,2,1,0:T(8,128)S(1)} copy-done((f32[16,3,32,256]{3,2,1,0:T(8,128)S(1)}, f32[16,3,32,256]{3,2,1,0:T(8,128)}, u32[]{:S(2)}) %copy-start) | copy-done | bytes 1572888
  2.0 0.0 copy-start.1
  2.0 0.9 %copy-done.1 = f32[3,32,256]{2,1,0:T(8,128)S(1)} copy-done((f32[3,32,256]{2,1,0:T(8,128)S(1)}, f32[3,32,256]{2,1,0:T(8,128)}, u32[]{:S(2)}) %copy-start.1) | copy-done | bytes 98328
  2.9 67.5 %shard_map.41 = (f32[16,3,32,256]{3,2,1,0:T(8,128)S(1)}, f32[16,16]{1,0:T(8,128)S(1)}) custom-call(f32[3,32,256]{2,1,0:T(8,128)S(1)} %copy-done.1, f32[16,3,32,256]{3,2,1,0:T(8,128)S(1)} %copy-done), custom_call_target="tpu_custom_call" | custom-call | tf_op jit(solution)/shard_map/pallas_call | solution.py:314
  70.4 1.1 %copy.6 = f32[16,3,32,256]{3,2,1,0:T(8,128)} copy(f32[16,3,32,256]{3,2,1,0:T(8,128)S(1)} %get-tuple-element.4) | data formatting | bytes 3145728
  71.6 0.6 copy.7
Async XLA Ops:
  0.6 1.4 %copy-start = (f32[16,3,32,256]{3,2,1,0:T(8,128)S(1)}, f32[16,3,32,256]{3,2,1,0:T(8,128)}, u32[]{:S(2)}) copy-start(f32[16,3,32,256]{3,2,1,0:T(8,128)} %perts_hbm.1) | copy-start | bytes 4718596
  2.0 0.9 %copy-start.1 = (f32[3,32,256]{2,1,0:T(8,128)S(1)}, f32[3,32,256]{2,1,0:T(8,128)}, u32[]{:S(2)}) copy-start(f32[3,32,256]{2,1,0:T(8,128)} %ctrl_hbm.1) | copy-start | bytes 294916
where the time goes:
time: 72.4 us; the launch traced here: 72.2 us
  Pallas kernels  67.5 us (93%)
  local copies, waits for them, and re-layouts  4.04 us (6%)
    pallas_call x1, Pallas kernels, body(): pl.pallas_call(functools.partial(kernel, nx_dev, ny_dev, members, rows, c...  67.5 us
    unnamed x6, local copies, waits for them, and re-layouts  4.04 us

commit v1 on v0

v1 whole, which is shorter than its diff:
```python
import functools
import math

import jax
import jax.numpy as jnp
from jax import lax
from jax.experimental import pallas as pl
from jax.experimental.pallas import tpu as pltpu
from jax.sharding import PartitionSpec as P

MESH = pl.DeviceIdType.MESH
HALO = 8
STEPS = 2
MEAN_DEPTH = 4.0
TIME_STEP = 0.1
SCALE = TIME_STEP * (2.0 / 3.0)
HIGHEST = lax.Precision.HIGHEST


def kernel(
    nx_dev, ny_dev, members, rows, cols,
    ctrl_hbm, perts_hbm, basis_ref, rfac_ref,
    st, pk, halo, nat, band, now, mid, cini, cfin, cor, fin, parts, red1, red2,
    in_sem, y_send, y_recv, x_send, x_recv, r1_send, r1_recv, r2_send, r2_recv,
):
    gx, gy = lax.axis_index("gx"), lax.axis_index("gy")
    ext = rows + 2 * HALO
    tall = ext // 8
    pairs = members // 2 + 1
    lane = lax.broadcasted_iota(jnp.int32, (8, 128), 1)
    sub = lax.broadcasted_iota(jnp.int32, (8, 128), 0)
    left, right = lax.rem(gx + nx_dev - 1, nx_dev), lax.rem(gx + 1, nx_dev)
    up, down = lax.rem(gy + ny_dev - 1, ny_dev), lax.rem(gy + 1, ny_dev)

    def own_copy(k):
        source = ctrl_hbm if k == 0 else perts_hbm.at[pl.ds((k - 1) * 4, 4)]
        target = st.at[0] if k == 0 else st.at[pl.ds((k - 1) * 4 + 1, 4)]
        if k == 0:
            return pltpu.make_async_copy(source, target.at[:, pl.ds(HALO, rows), :], in_sem.at[k])
        return pltpu.make_async_copy(source, target.at[:, :, pl.ds(HALO, rows), :], in_sem.at[k])

    for k in range(members // 4 + 1):
        own_copy(k).start()

    barrier = pltpu.get_barrier_semaphore()
    greeted = []
    for d in range(1, nx_dev):
        greeted.append((lax.rem(gx + d, nx_dev), gy))
    for d in range(1, ny_dev):
        greeted.append((gx, lax.rem(gy + d, ny_dev)))
    for a in (left, right):
        for b in (up, down):
            greeted.append((a, b))
    for peer in greeted:
        pl.semaphore_signal(barrier, inc=1, device_id=peer, device_id_type=MESH)

    grid_rows = rows * ny_dev
    for t in range(tall):
        row = lax.rem(gy * rows - HALO + tall * sub + t + grid_rows, grid_rows).astype(jnp.float32)
        cor[t] = TIME_STEP * 0.5 * (1.0 + 0.5 * jnp.sin(2.0 * math.pi * row / float(grid_rows)))
    cini[...] = jnp.zeros_like(cini)
    cfin[...] = jnp.zeros_like(cfin)

    for k in range(members // 4 + 1):
        own_copy(k).wait()

    wide = lax.broadcasted_iota(jnp.int32, (rows, 128), 1) // 8

    @pl.loop(0, 3)
    def _(f):
        first = jnp.zeros((rows, 128), jnp.float32)
        last = jnp.zeros((rows, 128), jnp.float32)
        for m in range(members):
            head = st[m + 1, f, HALO : HALO + rows, 0:128]
            tail = st[m + 1, f, HALO : HALO + rows, cols - 128 : cols]
            both = pltpu.roll(jnp.where(wide < 8, head, tail), (8 * m) % 128, 1)
            first = jnp.where(wide == m, both, first)
            last = jnp.where(wide == (m + 15) % 16, both, last)
        pk[0, 0, f] = first
        pk[1, 0, f] = last
        pk[0, 1, f] = st[0, f, HALO : HALO + rows, 0:128]
        pk[1, 1, f] = st[0, f, HALO : HALO + rows, cols - 128 : cols]

    def x_copies():
        out = []
        for side, x_to in ((0, left), (1, right)):
            for place, (start, count, to, y_to) in enumerate(
                ((0, rows, HALO, gy), (0, HALO, HALO + rows, up), (rows - HALO, HALO, 0, down))
            ):
                out.append(
                    pltpu.make_async_remote_copy(
                        pk.at[side, :, :, pl.ds(start, count), :],
                        halo.at[side, :, :, pl.ds(to, count), :],
                        x_send.at[side, place], x_recv.at[side, place],
                        device_id=(x_to, y_to), device_id_type=MESH)
                )
        return out

    pl.semaphore_wait(barrier, len(greeted))
    for copy in x_copies():
        copy.start()

    def y_copies(p, field_ref, st_ref):
        lead = (slice(None),) * (len(field_ref.shape) - 2)
        return [
            pltpu.make_async_remote_copy(
                field_ref.at[lead + (pl.ds(start, HALO),)],
                st_ref.at[lead + (pl.ds(to, HALO),)],
                y_send.at[way, p], y_recv.at[way, p], device_id=(gx, y_to), device_id_type=MESH)
            for way, (start, to, y_to) in enumerate(((0, HALO + rows, up), (rows - HALO, 0, down)))
        ]

    def control_y():
        return y_copies(0, ctrl_hbm, st.at[0])

    def pair_y(p):
        return y_copies(p, perts_hbm.at[pl.ds(2 * p - 2, 2)], st.at[pl.ds(2 * p - 1, 2)])

    for copy in control_y():
        copy.start()

    @pl.loop(1, pairs)
    def _(p):
        for copy in pair_y(p):
            copy.start()

    for copy in x_copies():
        copy.wait()

    k_id = lax.rem(lax.broadcasted_iota(jnp.int32, (256, 128), 0), 128)
    ahead = lax.rem(k_id - lax.broadcasted_iota(jnp.int32, (256, 128), 1) + 128, 128)
    weights = jnp.where(ahead == 1, 1.0, jnp.where(ahead == 127, -1.0, 0.0))
    weights = jnp.where(ahead == 2, -0.125, jnp.where(ahead == 126, 0.125, weights))
    band[...] = weights.astype(jnp.bfloat16)

    def put(ref, f, i, t, value):
        ref[f, i, t + 2] = value
        if t < 2:
            ref[f, i, t + 2 + tall] = pltpu.roll(value, 7, 0)
        if t >= tall - 2:
            ref[f, i, t + 2 - tall] = pltpu.roll(value, 1, 0)

    def put_state(ref, i, t, h, e, n):
        put(ref, 0, i, t, h)
        put(ref, 1, i, t, e)
        put(ref, 2, i, t, n)
        put(ref, 3, i, t, (SCALE * SCALE * MEAN_DEPTH + h) * n)

    def slopes_x(ref, i):
        h, e, n = (ref[f, i, 2 : 2 + tall].reshape(ext, 128) for f in range(3))
        z = jnp.concatenate([h, e, n, (SCALE * SCALE * MEAN_DEPTH + h) * e], axis=0)
        top = z.astype(jnp.bfloat16)
        rest = (z - top.astype(jnp.float32)).astype(jnp.bfloat16)
        out = jnp.dot(jnp.concatenate([top, rest], axis=1), band[...], preferred_element_type=jnp.float32)
        return out.reshape(4, tall, 8, 128)

    def slope_y(ref, f, i, t):
        return (ref[f, i, t + 3] - ref[f, i, t + 1]) - 0.125 * (ref[f, i, t + 4] - ref[f, i, t])

    def forward(ref, i, t, along):
        h, e, n = ref[0, i, t + 2], ref[1, i, t + 2], ref[2, i, t + 2]
        c = cor[t]
        new_h = h - along[3, t] - slope_y(ref, 3, i, t)
        new_e = e - (e * along[1, t] + n * slope_y(ref, 1, i, t) + along[0, t]) + c * n
        new_n = n - (e * along[2, t] + n * slope_y(ref, 2, i, t) + slope_y(ref, 0, i, t)) - c * e
        return new_h, new_e, new_n

    @pl.loop(0, pairs)
    def _(p):
        @pl.when(p == 0)
        def _():
            for copy in control_y():
                copy.wait_recv()

        @pl.when(p > 0)
        def _():
            for copy in pair_y(p):
                copy.wait_recv()

        slot = jnp.where(p == 0, 1, 0)
        first = jnp.maximum(2 * p - 1, 0)
        for s, k in enumerate((first, 2 * p)):
            for f in range(3):
                for i in range(2):
                    nat[s, f, i] = st[k, f, :, 128 * i : 128 * (i + 1)]
        places = (jnp.maximum(first - 1, 0), jnp.maximum(2 * p - 1, 0))
        for f in range(3):
            scale = SCALE * SCALE if f == 0 else SCALE
            for t in range(tall):
                pick = pl.ds(t, 8, stride=tall)
                after, before = halo[0, slot, f, pick, :], halo[1, slot, f, pick, :]
                rings, middle = [], []
                for s, m in enumerate(places):
                    low, high = nat[s, f, 0, pick, :], nat[s, f, 1, pick, :]
                    beyond = pltpu.roll(jnp.where(lane // 8 == m, after, before), lax.rem(128 - 8 * m, 128), 1)
                    rings.append(jnp.where(lane < 120, low, beyond))
                    rings.append(jnp.where(lane < 8, beyond, high))
                    middle.append(jnp.where(lane < 64, high, low))
                apart = pltpu.roll(middle[1], 64, 1)
                rings.append(jnp.where((lane < 32) | (lane >= 96), middle[0], apart))
                for i in range(5):
                    now[f, i, t + 2] = cini[f, i, t] + scale * rings[i]

        @pl.when(p == 0)
        def _():
            for f in range(3):
                cini[f] = now[f, :, 2 : 2 + tall]

        for i in range(5):
            for t in range(tall):
                put_state(now, i, t, now[0, i, t + 2], now[1, i, t + 2], now[2, i, t + 2])

        @pl.loop(0, STEPS)
        def _(step):
            for i in range(5):
                along = slopes_x(now, i)
                for t in range(tall):
                    put_state(mid, i, t, *forward(now, i, t, along))
            for i in range(5):
                along = slopes_x(mid, i)
                for t in range(tall):
                    new = forward(mid, i, t, along)
                    put_state(now, i, t, *(0.5 * (now[f, i, t + 2] + new[f]) for f in range(3)))

        for f in range(3):
            scale = 1.0 / (SCALE * SCALE) if f == 0 else 1.0 / SCALE
            for t in range(tall):
                z = [scale * (now[f, i, t + 2] - cfin[f, i, t]) for i in range(5)]
                pick = pl.ds(t, 8, stride=tall)
                for s, k in enumerate((first, 2 * p)):
                    both = z[4] if s == 0 else pltpu.roll(z[4], 64, 1)
                    fin[k, f, 0, pick, :] = jnp.where(lane < 112, z[2 * s], both)
                    fin[k, f, 1, pick, :] = jnp.where(lane < 16, both, z[2 * s + 1])

        @pl.when(p == 0)
        def _():
            for f in range(3):
                cfin[f] = now[f, :, 2 : 2 + tall]

    for copy in control_y():
        copy.wait_send()

    @pl.loop(1, pairs)
    def _(p):
        for copy in pair_y(p):
            copy.wait_send()

    block = 8 * members

    def piece(f, r):
        both = [fin[1:, f, i, pl.ds(pl.multiple_of(HALO + 8 * r, 8), 8), :].reshape(block, 128) for i in range(2)]
        return jnp.concatenate(both, axis=1)

    def add_piece(j, total):
        x = piece(j // (rows // 8), lax.rem(j, rows // 8))
        top = x.astype(jnp.bfloat16)
        rest = (x - top.astype(jnp.float32)).astype(jnp.bfloat16)
        x = jnp.concatenate([top, rest], axis=0)
        parts[j] = x
        return total + lax.dot_general(x, x, (((1,), (1,)), ((), ())), preferred_element_type=jnp.float32)

    pieces = 3 * rows // 8
    total = lax.fori_loop(0, pieces, add_piece, jnp.zeros((2 * block, 2 * block), jnp.float32))
    total = total[:block] + total[block:]
    total = total[:, :block] + total[:, block:]
    r_id = lax.broadcasted_iota(jnp.int32, (block, block), 0)
    c_id = lax.broadcasted_iota(jnp.int32, (block, block), 1)
    same = lax.rem(r_id, 8) == lax.rem(c_id, 8)
    total = jnp.where(same, total, 0.0)
    total = jnp.sum(total.reshape(members, 8, block), axis=1)
    g_id = lax.broadcasted_iota(jnp.int32, (block, 128), 0) // 8
    l_id = lax.broadcasted_iota(jnp.int32, (block, 128), 1)
    gather = jnp.where(g_id == l_id, 1.0, 0.0)
    gram = jnp.dot(total, gather, precision=HIGHEST, preferred_element_type=jnp.float32)

    def all_sum(value, buf, me, count, peer_of, send, recv):
        buf[me] = value
        copies = []
        for d in range(1, count):
            copies.append(
                pltpu.make_async_remote_copy(
                    buf.at[me], buf.at[me], send.at[d], recv.at[d],
                    device_id=peer_of(lax.rem(me + d, count)), device_id_type=MESH)
            )
        for copy in copies:
            copy.start()
        for copy in copies:
            copy.wait_recv()
        out = buf[0]
        for d in range(1, count):
            out = out + buf[d]
        return out, copies

    packed = jnp.where(lane < members, gram[0:8], pltpu.roll(gram[8:16], members, 1))
    packed, sent1 = all_sum(packed, red1, gx, nx_dev, lambda i: (i, gy), r1_send, r1_recv)
    packed, sent2 = all_sum(packed, red2, gy, ny_dev, lambda i: (gx, i), r2_send, r2_recv)
    for copy in sent1 + sent2:
        copy.wait_send()
    gram = jnp.concatenate([packed, pltpu.roll(packed, 128 - members, 1)], axis=0)

    row_id = lax.broadcasted_iota(jnp.int32, (members, 128), 0)
    col_id = lax.broadcasted_iota(jnp.int32, (members, 128), 1)
    work = jnp.where(col_id < members, gram, jnp.where(col_id - members == row_id, 1.0, 0.0))
    for k in range(members):
        column = jnp.sum(jnp.where(col_id == k, work, 0.0), axis=1, keepdims=True)
        pivot = jnp.sqrt(column[k : k + 1])
        row = work[k : k + 1] / pivot
        factor = column / pivot
        work = jnp.where(row_id > k, work - factor * row, jnp.where(row_id == k, row, work))
    length = float(3 * grid_rows * cols * nx_dev)
    rfac_ref[...] = jnp.where(row_id <= col_id, work * (1.0 / math.sqrt(length)), 0.0)[:, :members]

    inverse = pltpu.roll(work, 128 - members, 1) * math.sqrt(length)
    s_id = lax.broadcasted_iota(jnp.int32, (128, block), 0)
    e_id = lax.broadcasted_iota(jnp.int32, (128, block), 1) // 8
    spread = jnp.where(s_id == e_id, 1.0, 0.0)
    big = jnp.dot(inverse, spread, precision=HIGHEST, preferred_element_type=jnp.float32)
    big = jnp.broadcast_to(big[:, None, :], (members, 8, block)).reshape(block, block)
    big = jnp.where(same & (r_id // 8 >= c_id // 8), big, 0.0)

    top = big.astype(jnp.bfloat16)
    rest = (big - top.astype(jnp.float32)).astype(jnp.bfloat16)
    big = jnp.concatenate([jnp.concatenate([top, top], axis=1), jnp.concatenate([rest, rest], axis=1)], axis=0)

    @pl.loop(0, pieces)
    def _(j):
        f, r = j // (rows // 8), lax.rem(j, rows // 8)
        y = jnp.dot(big, parts[j], preferred_element_type=jnp.float32)
        y = y[:block] + y[block:]
        basis_ref[:, f, pl.ds(pl.multiple_of(8 * r, 8), 8), :] = y.reshape(members, 8, cols)


def body(control, perts):
    nx_dev, ny_dev = lax.axis_size("gx"), lax.axis_size("gy")
    members, _, rows, cols = perts.shape
    states, ext = members + 1, rows + 2 * HALO
    tall = ext // 8
    f32 = jnp.float32
    dma = pltpu.SemaphoreType.DMA
    return pl.pallas_call(
        functools.partial(kernel, nx_dev, ny_dev, members, rows, cols),
        out_shape=(
            jax.ShapeDtypeStruct(perts.shape, f32),
            jax.ShapeDtypeStruct((members, members), f32),
        ),
        in_specs=[pl.BlockSpec(memory_space=pl.ANY)] * 2,
        out_specs=[pl.BlockSpec(memory_space=pltpu.VMEM)] * 2,
        scratch_shapes=[
            pltpu.VMEM((states, 3, ext, cols), f32),
            pltpu.VMEM((2, 2, 3, rows, 128), f32),
            pltpu.VMEM((2, 2, 3, ext, 128), f32),
            pltpu.VMEM((2, 3, 2, ext, 128), f32),
            pltpu.VMEM((256, 128), jnp.bfloat16),
            pltpu.VMEM((4, 5, tall + 4, 8, 128), f32),
            pltpu.VMEM((4, 5, tall + 4, 8, 128), f32),
            pltpu.VMEM((3, 5, tall, 8, 128), f32),
            pltpu.VMEM((3, 5, tall, 8, 128), f32),
            pltpu.VMEM((tall, 8, 128), f32),
            pltpu.VMEM((states, 3, 2, ext, 128), f32),
            pltpu.VMEM((3 * rows // 8, 16 * members, cols), jnp.bfloat16),
            pltpu.VMEM((nx_dev, 8, 128), f32),
            pltpu.VMEM((ny_dev, 8, 128), f32),
            dma((members // 4 + 1,)),
            dma((2, members // 2 + 1)),
            dma((2, members // 2 + 1)),
            dma((2, 3)),
            dma((2, 3)),
            dma((nx_dev,)),
            dma((nx_dev,)),
            dma((ny_dev,)),
            dma((ny_dev,)),
        ],
        compiler_params=pltpu.CompilerParams(
            collective_id=0, has_side_effects=True, vmem_limit_bytes=60 * 1024 * 1024
        ),
    )(control, perts)


def solution(mesh):
    in_specs = (P(None, "gy", "gx"), P(None, None, "gy", "gx"))
    out_specs = (P(None, None, "gy", "gx"), P())
    return jax.shard_map(body, mesh=mesh, in_specs=in_specs, out_specs=out_specs, check_vma=False)
```

time: 72.4 us -> 49.3 us (0.68)
  Pallas kernels: 67.5 us -> 45.2 us
    pallas_call x1, Pallas kernels: 67.5 us -> 45.2 us  [body(): pl.pallas_call(functools.partial(kernel, nx_dev, ny_dev, members, rows, c...]
    unnamed x6 -> x4, local copies, waits for them, and re-layouts: 4.04 us -> 3.34 us
where the time goes in v1:
time: 49.3 us; the launch traced here: 49.2 us
  Pallas kernels  45.2 us (92%)
  local copies, waits for them, and re-layouts  3.34 us (7%)
  between operations  0.65 us (1%)
    pallas_call x1, Pallas kernels, body(): pl.pallas_call(functools.partial(kernel, nx_dev, ny_dev, members, rows, c...  45.2 us
    unnamed x4, local copies, waits for them, and re-layouts  3.34 us

profile of v1, /device:TPU:1, one launch (start us, length us, event | category | flops | bytes accessed | tf_op | source)
XLA Modules:
  0.0 49.2 jit_solution(9146716259036010727)
XLA Ops:
  0.6 45.2 %shard_map.41 = (f32[16,3,32,256]{3,2,1,0:T(8,128)}, f32[16,16]{1,0:T(8,128)}) custom-call(f32[3,32,256]{2,1,0:T(8,128)} %ctrl_hbm.1, f32[16,3,32,256]{3,2,1,0:T(8,128)} %perts_hbm.1), custom_call_target="tpu_custom_call" | custom-call | tf_op jit(solution)/shard_map/pallas_call | solution.py:340
  45.8 0.0 copy-start
  45.8 2.7 %copy.6 = f32[16,3,32,256]{3,2,1,0:T(8,128)} copy(f32[16,3,32,256]{3,2,1,0:T(8,128)} %get-tuple-element.4) | data formatting | bytes 3145728
  48.6 0.0 copy-done
  48.6 0.6 %copy.7 = f32[16,16]{1,0:T(8,128)} copy(f32[16,16]{1,0:T(8,128)S(1)} %copy-done) | data formatting | bytes 2048
Async XLA Ops:
  45.8 2.7 %copy-start = (f32[16,16]{1,0:T(8,128)S(1)}, f32[16,16]{1,0:T(8,128)}, u32[]{:S(2)}) copy-start(f32[16,16]{1,0:T(8,128)} %get-tuple-element.5) | copy-start | bytes 3076

commit v2 on v1

--- a/solution.py
+++ b/solution.py
@@ -14,13 +14,12 @@
 MEAN_DEPTH = 4.0
 TIME_STEP = 0.1
 SCALE = TIME_STEP * (2.0 / 3.0)
-HIGHEST = lax.Precision.HIGHEST
 
 
 def kernel(
     nx_dev, ny_dev, members, rows, cols,
-    ctrl_hbm, perts_hbm, basis_ref, rfac_ref,
-    st, pk, halo, nat, band, now, mid, cini, cfin, cor, fin, parts, red1, red2,
+    ctrl_hbm, perts_hbm, fin, factor_ref,
+    st, pk, halo, nat, band, now, mid, cini, cfin, cor, parts, red1, red2,
     in_sem, y_send, y_recv, x_send, x_recv, r1_send, r1_recv, r2_send, r2_recv,
 ):
     gx, gy = lax.axis_index("gx"), lax.axis_index("gy")
@@ -58,7 +57,8 @@
     for t in range(tall):
         row = lax.rem(gy * rows - HALO + tall * sub + t + grid_rows, grid_rows).astype(jnp.float32)
         cor[t] = TIME_STEP * 0.5 * (1.0 + 0.5 * jnp.sin(2.0 * math.pi * row / float(grid_rows)))
-    cini[...] = jnp.zeros_like(cini)
+    for f in range(3):
+        cini[f] = jnp.full(cini.shape[1:], SCALE * SCALE * MEAN_DEPTH if f == 0 else 0.0, jnp.float32)
     cfin[...] = jnp.zeros_like(cfin)
 
     for k in range(members // 4 + 1):
@@ -125,7 +125,7 @@
             copy.start()
 
     for copy in x_copies():
-        copy.wait()
+        copy.wait_recv()
 
     k_id = lax.rem(lax.broadcasted_iota(jnp.int32, (256, 128), 0), 128)
     ahead = lax.rem(k_id - lax.broadcasted_iota(jnp.int32, (256, 128), 1) + 128, 128)
@@ -144,11 +144,11 @@
         put(ref, 0, i, t, h)
         put(ref, 1, i, t, e)
         put(ref, 2, i, t, n)
-        put(ref, 3, i, t, (SCALE * SCALE * MEAN_DEPTH + h) * n)
+        put(ref, 3, i, t, h * n)
 
     def slopes_x(ref, i):
         h, e, n = (ref[f, i, 2 : 2 + tall].reshape(ext, 128) for f in range(3))
-        z = jnp.concatenate([h, e, n, (SCALE * SCALE * MEAN_DEPTH + h) * e], axis=0)
+        z = jnp.concatenate([h, e, n, h * e], axis=0)
         top = z.astype(jnp.bfloat16)
         rest = (z - top.astype(jnp.float32)).astype(jnp.bfloat16)
         out = jnp.dot(jnp.concatenate([top, rest], axis=1), band[...], preferred_element_type=jnp.float32)
@@ -237,7 +237,7 @@
             for f in range(3):
                 cfin[f] = now[f, :, 2 : 2 + tall]
 
-    for copy in control_y():
+    for copy in x_copies() + control_y():
         copy.wait_send()
 
     @pl.loop(1, pairs)
@@ -245,33 +245,30 @@
         for copy in pair_y(p):
             copy.wait_send()
 
-    block = 8 * members
-
-    def piece(f, r):
-        both = [fin[1:, f, i, pl.ds(pl.multiple_of(HALO + 8 * r, 8), 8), :].reshape(block, 128) for i in range(2)]
-        return jnp.concatenate(both, axis=1)
-
-    def add_piece(j, total):
-        x = piece(j // (rows // 8), lax.rem(j, rows // 8))
-        top = x.astype(jnp.bfloat16)
-        rest = (x - top.astype(jnp.float32)).astype(jnp.bfloat16)
-        x = jnp.concatenate([top, rest], axis=0)
-        parts[j] = x
-        return total + lax.dot_general(x, x, (((1,), (1,)), ((), ())), preferred_element_type=jnp.float32)
-
-    pieces = 3 * rows // 8
-    total = lax.fori_loop(0, pieces, add_piece, jnp.zeros((2 * block, 2 * block), jnp.float32))
-    total = total[:block] + total[block:]
-    total = total[:, :block] + total[:, block:]
-    r_id = lax.broadcasted_iota(jnp.int32, (block, block), 0)
-    c_id = lax.broadcasted_iota(jnp.int32, (block, block), 1)
-    same = lax.rem(r_id, 8) == lax.rem(c_id, 8)
-    total = jnp.where(same, total, 0.0)
-    total = jnp.sum(total.reshape(members, 8, block), axis=1)
-    g_id = lax.broadcasted_iota(jnp.int32, (block, 128), 0) // 8
-    l_id = lax.broadcasted_iota(jnp.int32, (block, 128), 1)
-    gather = jnp.where(g_id == l_id, 1.0, 0.0)
-    gram = jnp.dot(total, gather, precision=HIGHEST, preferred_element_type=jnp.float32)
+    @pl.loop(0, members // 4)
+    def _(a):
+        @pl.loop(0, a + 1)
+        def _(b):
+            total = [[None] * 4 for _ in range(4)]
+            for f in range(3):
+                for i in range(2):
+                    x = [fin[1 + 4 * a + u, f, i, HALO : HALO + rows, :] for u in range(4)]
+                    y = [fin[1 + 4 * b + u, f, i, HALO : HALO + rows, :] for u in range(4)]
+                    for u in range(4):
+                        for v in range(4):
+                            z = jnp.sum((x[u] * y[v]).reshape(rows // 8, 8, 128), axis=0)
+                            total[u][v] = z if total[u][v] is None else total[u][v] + z
+            for u in range(4):
+                for v in range(4):
+                    parts[4 * a + u, 4 * b + v] = total[u][v]
+                    parts[4 * b + v, 4 * a + u] = total[u][v]
+
+    row_id = lax.broadcasted_iota(jnp.int32, (members, 128), 0)
+    col_id = lax.broadcasted_iota(jnp.int32, (members, 128), 1)
+    gram = jnp.zeros((members, 128), jnp.float32)
+    for m in range(members):
+        sums = jnp.sum(jnp.sum(parts[m], axis=1), axis=1, keepdims=True)
+        gram = jnp.where(col_id == m, sums, gram)
 
     def all_sum(value, buf, me, count, peer_of, send, recv):
         buf[me] = value
@@ -298,36 +295,38 @@
         copy.wait_send()
     gram = jnp.concatenate([packed, pltpu.roll(packed, 128 - members, 1)], axis=0)
 
-    row_id = lax.broadcasted_iota(jnp.int32, (members, 128), 0)
-    col_id = lax.broadcasted_iota(jnp.int32, (members, 128), 1)
     work = jnp.where(col_id < members, gram, jnp.where(col_id - members == row_id, 1.0, 0.0))
+    pivots = jnp.ones((members, 1), jnp.float32)
     for k in range(members):
-        column = jnp.sum(jnp.where(col_id == k, work, 0.0), axis=1, keepdims=True)
-        pivot = jnp.sqrt(column[k : k + 1])
-        row = work[k : k + 1] / pivot
-        factor = column / pivot
-        work = jnp.where(row_id > k, work - factor * row, jnp.where(row_id == k, row, work))
-    length = float(3 * grid_rows * cols * nx_dev)
-    rfac_ref[...] = jnp.where(row_id <= col_id, work * (1.0 / math.sqrt(length)), 0.0)[:, :members]
-
-    inverse = pltpu.roll(work, 128 - members, 1) * math.sqrt(length)
-    s_id = lax.broadcasted_iota(jnp.int32, (128, block), 0)
-    e_id = lax.broadcasted_iota(jnp.int32, (128, block), 1) // 8
-    spread = jnp.where(s_id == e_id, 1.0, 0.0)
-    big = jnp.dot(inverse, spread, precision=HIGHEST, preferred_element_type=jnp.float32)
-    big = jnp.broadcast_to(big[:, None, :], (members, 8, block)).reshape(block, block)
-    big = jnp.where(same & (r_id // 8 >= c_id // 8), big, 0.0)
-
-    top = big.astype(jnp.bfloat16)
-    rest = (big - top.astype(jnp.float32)).astype(jnp.bfloat16)
-    big = jnp.concatenate([jnp.concatenate([top, top], axis=1), jnp.concatenate([rest, rest], axis=1)], axis=0)
-
-    @pl.loop(0, pieces)
-    def _(j):
-        f, r = j // (rows // 8), lax.rem(j, rows // 8)
-        y = jnp.dot(big, parts[j], preferred_element_type=jnp.float32)
-        y = y[:block] + y[block:]
-        basis_ref[:, f, pl.ds(pl.multiple_of(8 * r, 8), 8), :] = y.reshape(members, 8, cols)
+        column = work[:, k : k + 1]
+        pivot = column[k : k + 1]
+        work = work - jnp.where(row_id > k, column, 0.0) * (work[k : k + 1] * (1.0 / pivot))
+        pivots = jnp.where(row_id[:, :1] == k, pivot, pivots)
+    factor_ref[...] = work / jnp.sqrt(pivots)
+
+
+def apply_kernel(length, members, rows, bred, factor, basis_hbm, rfac_hbm, table, out, rout, sem):
+    row_id = lax.broadcasted_iota(jnp.int32, (members, members), 0)
+    col_id = lax.broadcasted_iota(jnp.int32, (members, members), 1)
+    rout[...] = jnp.where(row_id <= col_id, factor[:, :members] * (1.0 / math.sqrt(length)), 0.0)
+    small = pltpu.make_async_copy(rout, rfac_hbm, sem.at[3])
+    small.start()
+    for j in range(members):
+        column = factor[:, members + j : members + j + 1] * math.sqrt(length)
+        table[j] = jnp.broadcast_to(column, (members, 128))
+    copies = []
+    for f in range(3):
+        for i in range(2):
+            x = [bred[1 + j, f, i, HALO : HALO + rows, :] for j in range(members)]
+            for m in range(members):
+                total = table[0, m : m + 1, :] * x[0]
+                for j in range(1, m + 1):
+                    total = total + table[j, m : m + 1, :] * x[j]
+                out[m, f, :, 128 * i : 128 * (i + 1)] = total
+        copies.append(pltpu.make_async_copy(out.at[:, pl.ds(f, 1)], basis_hbm.at[:, pl.ds(f, 1)], sem.at[f]))
+        copies[-1].start()
+    for copy in copies + [small]:
+        copy.wait()
 
 
 def body(control, perts):
@@ -337,14 +336,15 @@
     tall = ext // 8
     f32 = jnp.float32
     dma = pltpu.SemaphoreType.DMA
-    return pl.pallas_call(
+    vmem, hbm = pl.BlockSpec(memory_space=pltpu.VMEM), pl.BlockSpec(memory_space=pltpu.HBM)
+    bred, factor = pl.pallas_call(
         functools.partial(kernel, nx_dev, ny_dev, members, rows, cols),
         out_shape=(
-            jax.ShapeDtypeStruct(perts.shape, f32),
-            jax.ShapeDtypeStruct((members, members), f32),
+            jax.ShapeDtypeStruct((states, 3, 2, ext, 128), f32),
+            jax.ShapeDtypeStruct((members, 128), f32),
         ),
-        in_specs=[pl.BlockSpec(memory_space=pl.ANY)] * 2,
-        out_specs=[pl.BlockSpec(memory_space=pltpu.VMEM)] * 2,
+        in_specs=[hbm] * 2,
+        out_specs=[vmem] * 2,
         scratch_shapes=[
             pltpu.VMEM((states, 3, ext, cols), f32),
             pltpu.VMEM((2, 2, 3, rows, 128), f32),
@@ -356,8 +356,7 @@
             pltpu.VMEM((3, 5, tall, 8, 128), f32),
             pltpu.VMEM((3, 5, tall, 8, 128), f32),
             pltpu.VMEM((tall, 8, 128), f32),
-            pltpu.VMEM((states, 3, 2, ext, 128), f32),
-            pltpu.VMEM((3 * rows // 8, 16 * members, cols), jnp.bfloat16),
+            pltpu.VMEM((members, members, 8, 128), f32),
             pltpu.VMEM((nx_dev, 8, 128), f32),
             pltpu.VMEM((ny_dev, 8, 128), f32),
             dma((members // 4 + 1,)),
@@ -371,9 +370,26 @@
             dma((ny_dev,)),
         ],
         compiler_params=pltpu.CompilerParams(
-            collective_id=0, has_side_effects=True, vmem_limit_bytes=60 * 1024 * 1024
+            collective_id=0, has_side_effects=True, vmem_limit_bytes=24 * 1024 * 1024
         ),
     )(control, perts)
+    length = float(3 * rows * ny_dev * cols * nx_dev)
+    return pl.pallas_call(
+        functools.partial(apply_kernel, length, members, rows),
+        out_shape=(
+            jax.ShapeDtypeStruct(perts.shape, f32),
+            jax.ShapeDtypeStruct((members, members), f32),
+        ),
+        in_specs=[vmem] * 2,
+        out_specs=[hbm] * 2,
+        scratch_shapes=[
+            pltpu.VMEM((members, members, 128), f32),
+            pltpu.VMEM((members, 3, rows, cols), f32),
+            pltpu.VMEM((members, members), f32),
+            dma((4,)),
+        ],
+        compiler_params=pltpu.CompilerParams(vmem_limit_bytes=24 * 1024 * 1024),
+    )(bred, factor)
 
 
 def solution(mesh):

time: 49.3 us -> 44.3 us (0.90)
  Pallas kernels: 45.2 us -> 41.2 us
  local copies, waits for them, and re-layouts: 3.34 us -> 2.29 us
    pallas_call x1, Pallas kernels: 45.2 us -> 39.4 us  [body(): pl.pallas_call(functools.partial(kernel, nx_dev, ny_dev, members, rows, c...]
    pallas_call x0 -> x1, Pallas kernels: none -> 1.81 us  [body(): pl.pallas_call(functools.partial(apply_kernel, length, members, rows), ou...]
    unnamed x4, local copies, waits for them, and re-layouts: 3.34 us -> 2.29 us
where the time goes in v2:
time: 44.3 us; the launch traced here: 44.2 us
  Pallas kernels  41.2 us (93%)
  local copies, waits for them, and re-layouts  2.29 us (5%)
  between operations  0.65 us (1%)
    pallas_call x1, Pallas kernels, body(): pl.pallas_call(functools.partial(kernel, nx_dev, ny_dev, members, rows, c...  39.4 us
    unnamed x4, local copies, waits for them, and re-layouts  2.29 us
    pallas_call x1, Pallas kernels, body(): pl.pallas_call(functools.partial(apply_kernel, length, members, rows), ou...  1.81 us

profile of v2, /device:TPU:1, one launch (start us, length us, event | category | flops | bytes accessed | tf_op | source)
XLA Modules:
  0.0 44.2 jit_solution(8114569816885866561)
XLA Ops:
  0.6 0.0 copy-start
  0.6 1.4 %copy-done = f32[16,3,32,256]{3,2,1,0:T(8,128)S(1)} copy-done((f32[16,3,32,256]{3,2,1,0:T(8,128)S(1)}, f32[16,3,32,256]{3,2,1,0:T(8,128)}, u32[]{:S(2)}) %copy-start) | copy-done | bytes 1572888
  2.0 0.0 copy-start.1
  2.0 0.9 %copy-done.1 = f32[3,32,256]{2,1,0:T(8,128)S(1)} copy-done((f32[3,32,256]{2,1,0:T(8,128)S(1)}, f32[3,32,256]{2,1,0:T(8,128)}, u32[]{:S(2)}) %copy-start.1) | copy-done | bytes 98328
  2.9 39.4 %shard_map.41 = (f32[17,3,2,48,128]{4,3,2,1,0:T(8,128)S(1)}, f32[16,128]{1,0:T(8,128)S(1)}) custom-call(f32[3,32,256]{2,1,0:T(8,128)S(1)} %copy-done.1, f32[16,3,32,256]{3,2,1,0:T(8,128)S(1)} %copy-done), custom_call_target="tpu_custom_call" | custom-call | tf_op jit(solution)/shard_map/pallas_call | solution.py:340
  42.4 1.8 %shard_map.42 = (f32[16,3,32,256]{3,2,1,0:T(8,128)}, f32[16,16]{1,0:T(8,128)}) custom-call(f32[17,3,2,48,128]{4,3,2,1,0:T(8,128)S(1)} %get-tuple-element.4.bred, f32[16,128]{1,0:T(8,128)S(1)} %get-tuple-element.5.factor), custom_call_target="tpu_custom_call" | custom-call | tf_op jit(solution)/shard_map/pallas_call | solution.py:377
Async XLA Ops:
  0.6 1.4 %copy-start = (f32[16,3,32,256]{3,2,1,0:T(8,128)S(1)}, f32[16,3,32,256]{3,2,1,0:T(8,128)}, u32[]{:S(2)}) copy-start(f32[16,3,32,256]{3,2,1,0:T(8,128)} %perts_hbm.1) | copy-start | bytes 4718596
  2.0 0.9 %copy-start.1 = (f32[3,32,256]{2,1,0:T(8,128)S(1)}, f32[3,32,256]{2,1,0:T(8,128)}, u32[]{:S(2)}) copy-start(f32[3,32,256]{2,1,0:T(8,128)} %ctrl_hbm.1) | copy-start | bytes 294916

commit v3 on v2

--- a/solution.py
+++ b/solution.py
@@ -18,16 +18,14 @@
 
 def kernel(
     nx_dev, ny_dev, members, rows, cols,
-    ctrl_hbm, perts_hbm, fin, factor_ref,
-    st, pk, halo, nat, band, now, mid, cini, cfin, cor, parts, red1, red2,
-    in_sem, y_send, y_recv, x_send, x_recv, r1_send, r1_recv, r2_send, r2_recv,
+    ctrl_hbm, perts_hbm, bred_hbm, factor_ref,
+    st, pk, halo, band, now, mid, cini, cfin, cor, fin, parts, red1, red2,
+    in_sem, out_sem, y_send, y_recv, x_send, x_recv, r1_send, r1_recv, r2_send, r2_recv,
 ):
     gx, gy = lax.axis_index("gx"), lax.axis_index("gy")
     ext = rows + 2 * HALO
-    tall = ext // 8
     pairs = members // 2 + 1
     lane = lax.broadcasted_iota(jnp.int32, (8, 128), 1)
-    sub = lax.broadcasted_iota(jnp.int32, (8, 128), 0)
     left, right = lax.rem(gx + nx_dev - 1, nx_dev), lax.rem(gx + 1, nx_dev)
     up, down = lax.rem(gy + ny_dev - 1, ny_dev), lax.rem(gy + 1, ny_dev)
 
@@ -38,25 +36,21 @@
             return pltpu.make_async_copy(source, target.at[:, pl.ds(HALO, rows), :], in_sem.at[k])
         return pltpu.make_async_copy(source, target.at[:, :, pl.ds(HALO, rows), :], in_sem.at[k])
 
+    barrier = pltpu.get_barrier_semaphore()
+    greeted = [(a, b) for a in (left, right) for b in (gy, up, down)] + [(gx, up), (gx, down)]
+    greeted += [(lax.rem(gx + d, nx_dev), gy) for d in range(2, nx_dev - 1)]
+    greeted += [(gx, lax.rem(gy + d, ny_dev)) for d in range(2, ny_dev - 1)]
+    for peer in greeted[:8]:
+        pl.semaphore_signal(barrier, inc=1, device_id=peer, device_id_type=MESH)
     for k in range(members // 4 + 1):
         own_copy(k).start()
-
-    barrier = pltpu.get_barrier_semaphore()
-    greeted = []
-    for d in range(1, nx_dev):
-        greeted.append((lax.rem(gx + d, nx_dev), gy))
-    for d in range(1, ny_dev):
-        greeted.append((gx, lax.rem(gy + d, ny_dev)))
-    for a in (left, right):
-        for b in (up, down):
-            greeted.append((a, b))
-    for peer in greeted:
+    for peer in greeted[8:]:
         pl.semaphore_signal(barrier, inc=1, device_id=peer, device_id_type=MESH)
 
     grid_rows = rows * ny_dev
-    for t in range(tall):
-        row = lax.rem(gy * rows - HALO + tall * sub + t + grid_rows, grid_rows).astype(jnp.float32)
-        cor[t] = TIME_STEP * 0.5 * (1.0 + 0.5 * jnp.sin(2.0 * math.pi * row / float(grid_rows)))
+    row = gy * rows - HALO + grid_rows + lax.broadcasted_iota(jnp.int32, (ext, 128), 0)
+    row = lax.rem(row, grid_rows).astype(jnp.float32)
+    cor[...] = TIME_STEP * 0.5 * (1.0 + 0.5 * jnp.sin(2.0 * math.pi * row / float(grid_rows)))
     for f in range(3):
         cini[f] = jnp.full(cini.shape[1:], SCALE * SCALE * MEAN_DEPTH if f == 0 else 0.0, jnp.float32)
     cfin[...] = jnp.zeros_like(cfin)
@@ -133,37 +127,35 @@
     weights = jnp.where(ahead == 2, -0.125, jnp.where(ahead == 126, 0.125, weights))
     band[...] = weights.astype(jnp.bfloat16)
 
-    def put(ref, f, i, t, value):
-        ref[f, i, t + 2] = value
-        if t < 2:
-            ref[f, i, t + 2 + tall] = pltpu.roll(value, 7, 0)
-        if t >= tall - 2:
-            ref[f, i, t + 2 - tall] = pltpu.roll(value, 1, 0)
-
-    def put_state(ref, i, t, h, e, n):
-        put(ref, 0, i, t, h)
-        put(ref, 1, i, t, e)
-        put(ref, 2, i, t, n)
-        put(ref, 3, i, t, h * n)
-
-    def slopes_x(ref, i):
-        h, e, n = (ref[f, i, 2 : 2 + tall].reshape(ext, 128) for f in range(3))
-        z = jnp.concatenate([h, e, n, h * e], axis=0)
+    def put_state(ref, i, at, h, e, n):
+        for f, z in enumerate((h, e, n, h * n)):
+            ref[f, i, at : at + 8] = z
+
+    def slopes_x(ref, i, starts):
+        h, e, n = ([ref[f, i, at : at + 8] for at in starts] for f in range(3))
+        z = jnp.concatenate(h + e + n + [u * v for u, v in zip(h, e)], axis=0)
         top = z.astype(jnp.bfloat16)
         rest = (z - top.astype(jnp.float32)).astype(jnp.bfloat16)
         out = jnp.dot(jnp.concatenate([top, rest], axis=1), band[...], preferred_element_type=jnp.float32)
-        return out.reshape(4, tall, 8, 128)
-
-    def slope_y(ref, f, i, t):
-        return (ref[f, i, t + 3] - ref[f, i, t + 1]) - 0.125 * (ref[f, i, t + 4] - ref[f, i, t])
-
-    def forward(ref, i, t, along):
-        h, e, n = ref[0, i, t + 2], ref[1, i, t + 2], ref[2, i, t + 2]
-        c = cor[t]
-        new_h = h - along[3, t] - slope_y(ref, 3, i, t)
-        new_e = e - (e * along[1, t] + n * slope_y(ref, 1, i, t) + along[0, t]) + c * n
-        new_n = n - (e * along[2, t] + n * slope_y(ref, 2, i, t) + slope_y(ref, 0, i, t)) - c * e
+        return out.reshape(4, len(starts), 8, 128)
+
+    def slope_y(ref, f, i, at):
+        z = [ref[f, i, at + d : at + d + 8] for d in (-2, -1, 1, 2)]
+        return (z[2] - z[1]) - 0.125 * (z[3] - z[0])
+
+    def forward(ref, i, at, along):
+        h, e, n = (ref[f, i, at : at + 8] for f in range(3))
+        c = cor[at : at + 8]
+        new_h = h - along[3] - slope_y(ref, 3, i, at)
+        new_e = e - (e * along[1] + n * (slope_y(ref, 1, i, at) - c) + along[0])
+        new_n = n - (e * (along[2] + c) + n * slope_y(ref, 2, i, at) + slope_y(ref, 0, i, at))
         return new_h, new_e, new_n
+
+    def bred_out(p):
+        return pltpu.make_async_copy(fin.at[pl.ds(2 * p - 1, 2)], bred_hbm.at[pl.ds(2 * p - 2, 2)], out_sem.at[p])
+
+    inner = [list(range(2 * w, ext - 2 * w - 7, 8)) for w in (1, 2, 2, 4)]
+    inner[0].append(ext - 10)
 
     @pl.loop(0, pairs)
     def _(p):
@@ -179,19 +171,15 @@
 
         slot = jnp.where(p == 0, 1, 0)
         first = jnp.maximum(2 * p - 1, 0)
-        for s, k in enumerate((first, 2 * p)):
-            for f in range(3):
-                for i in range(2):
-                    nat[s, f, i] = st[k, f, :, 128 * i : 128 * (i + 1)]
         places = (jnp.maximum(first - 1, 0), jnp.maximum(2 * p - 1, 0))
         for f in range(3):
             scale = SCALE * SCALE if f == 0 else SCALE
-            for t in range(tall):
-                pick = pl.ds(t, 8, stride=tall)
+            for at in range(0, ext, 8):
+                pick = slice(at, at + 8)
                 after, before = halo[0, slot, f, pick, :], halo[1, slot, f, pick, :]
                 rings, middle = [], []
-                for s, m in enumerate(places):
-                    low, high = nat[s, f, 0, pick, :], nat[s, f, 1, pick, :]
+                for k, m in zip((first, 2 * p), places):
+                    low, high = st[k, f, pick, 0:128], st[k, f, pick, 128:256]
                     beyond = pltpu.roll(jnp.where(lane // 8 == m, after, before), lax.rem(128 - 8 * m, 128), 1)
                     rings.append(jnp.where(lane < 120, low, beyond))
                     rings.append(jnp.where(lane < 8, beyond, high))
@@ -199,51 +187,46 @@
                 apart = pltpu.roll(middle[1], 64, 1)
                 rings.append(jnp.where((lane < 32) | (lane >= 96), middle[0], apart))
                 for i in range(5):
-                    now[f, i, t + 2] = cini[f, i, t] + scale * rings[i]
+                    now[f, i, pick] = cini[f, i, pick] + scale * rings[i]
 
         @pl.when(p == 0)
         def _():
-            for f in range(3):
-                cini[f] = now[f, :, 2 : 2 + tall]
+            cini[...] = now[:3]
 
         for i in range(5):
-            for t in range(tall):
-                put_state(now, i, t, now[0, i, t + 2], now[1, i, t + 2], now[2, i, t + 2])
-
-        @pl.loop(0, STEPS)
-        def _(step):
+            for at in range(0, ext, 8):
+                now[3, i, at : at + 8] = now[0, i, at : at + 8] * now[2, i, at : at + 8]
+
+        for step in range(STEPS):
             for i in range(5):
-                along = slopes_x(now, i)
-                for t in range(tall):
-                    put_state(mid, i, t, *forward(now, i, t, along))
+                starts = inner[2 * step]
+                along = slopes_x(now, i, starts)
+                for j, at in enumerate(starts):
+                    put_state(mid, i, at, *forward(now, i, at, along[:, j]))
             for i in range(5):
-                along = slopes_x(mid, i)
-                for t in range(tall):
-                    new = forward(mid, i, t, along)
-                    put_state(now, i, t, *(0.5 * (now[f, i, t + 2] + new[f]) for f in range(3)))
+                starts = inner[2 * step + 1]
+                along = slopes_x(mid, i, starts)
+                for j, at in enumerate(starts):
+                    new = forward(mid, i, at, along[:, j])
+                    put_state(now, i, at, *(0.5 * (now[f, i, at : at + 8] + new[f]) for f in range(3)))
 
         for f in range(3):
             scale = 1.0 / (SCALE * SCALE) if f == 0 else 1.0 / SCALE
-            for t in range(tall):
-                z = [scale * (now[f, i, t + 2] - cfin[f, i, t]) for i in range(5)]
-                pick = pl.ds(t, 8, stride=tall)
+            for at in range(0, rows, 8):
+                pick, to = slice(HALO + at, HALO + at + 8), slice(at, at + 8)
+                z = [scale * (now[f, i, pick] - cfin[f, i, to]) for i in range(5)]
                 for s, k in enumerate((first, 2 * p)):
                     both = z[4] if s == 0 else pltpu.roll(z[4], 64, 1)
-                    fin[k, f, 0, pick, :] = jnp.where(lane < 112, z[2 * s], both)
-                    fin[k, f, 1, pick, :] = jnp.where(lane < 16, both, z[2 * s + 1])
+                    fin[k, f, 0, to, :] = jnp.where(lane < 112, z[2 * s], both)
+                    fin[k, f, 1, to, :] = jnp.where(lane < 16, both, z[2 * s + 1])
 
         @pl.when(p == 0)
         def _():
-            for f in range(3):
-                cfin[f] = now[f, :, 2 : 2 + tall]
-
-    for copy in x_copies() + control_y():
-        copy.wait_send()
-
-    @pl.loop(1, pairs)
-    def _(p):
-        for copy in pair_y(p):
-            copy.wait_send()
+            cfin[...] = now[:3, :, HALO : HALO + rows]
+
+        @pl.when(p > 0)
+        def _():
+            bred_out(p).start()
 
     @pl.loop(0, members // 4)
     def _(a):
@@ -252,8 +235,8 @@
             total = [[None] * 4 for _ in range(4)]
             for f in range(3):
                 for i in range(2):
-                    x = [fin[1 + 4 * a + u, f, i, HALO : HALO + rows, :] for u in range(4)]
-                    y = [fin[1 + 4 * b + u, f, i, HALO : HALO + rows, :] for u in range(4)]
+                    x = [fin[1 + 4 * a + u, f, i] for u in range(4)]
+                    y = [fin[1 + 4 * b + u, f, i] for u in range(4)]
                     for u in range(4):
                         for v in range(4):
                             z = jnp.sum((x[u] * y[v]).reshape(rows // 8, 8, 128), axis=0)
@@ -293,6 +276,18 @@
     packed, sent2 = all_sum(packed, red2, gy, ny_dev, lambda i: (gx, i), r2_send, r2_recv)
     for copy in sent1 + sent2:
         copy.wait_send()
+    @pl.loop(1, pairs)
+    def _(p):
+        bred_out(p).wait()
+
+    for copy in x_copies() + control_y():
+        copy.wait_send()
+
+    @pl.loop(1, pairs)
+    def _(p):
+        for copy in pair_y(p):
+            copy.wait_send()
+
     gram = jnp.concatenate([packed, pltpu.roll(packed, 128 - members, 1)], axis=0)
 
     work = jnp.where(col_id < members, gram, jnp.where(col_id - members == row_id, 1.0, 0.0))
@@ -305,7 +300,13 @@
     factor_ref[...] = work / jnp.sqrt(pivots)
 
 
-def apply_kernel(length, members, rows, bred, factor, basis_hbm, rfac_hbm, table, out, rout, sem):
+def apply_kernel(length, members, bred_hbm, factor_hbm, basis_hbm, rfac_hbm, bred, factor, table, out, rout, sem):
+    first = pltpu.make_async_copy(factor_hbm, factor, sem.at[4])
+    first.start()
+    parts = [pltpu.make_async_copy(bred_hbm.at[:, pl.ds(f, 1)], bred.at[:, pl.ds(f, 1)], sem.at[5 + f]) for f in range(3)]
+    for copy in parts:
+        copy.start()
+    first.wait()
     row_id = lax.broadcasted_iota(jnp.int32, (members, members), 0)
     col_id = lax.broadcasted_iota(jnp.int32, (members, members), 1)
     rout[...] = jnp.where(row_id <= col_id, factor[:, :members] * (1.0 / math.sqrt(length)), 0.0)
@@ -316,8 +317,9 @@
         table[j] = jnp.broadcast_to(column, (members, 128))
     copies = []
     for f in range(3):
+        parts[f].wait()
         for i in range(2):
-            x = [bred[1 + j, f, i, HALO : HALO + rows, :] for j in range(members)]
+            x = [bred[j, f, i] for j in range(members)]
             for m in range(members):
                 total = table[0, m : m + 1, :] * x[0]
                 for j in range(1, m + 1):
@@ -333,33 +335,33 @@
     nx_dev, ny_dev = lax.axis_size("gx"), lax.axis_size("gy")
     members, _, rows, cols = perts.shape
     states, ext = members + 1, rows + 2 * HALO
-    tall = ext // 8
     f32 = jnp.float32
     dma = pltpu.SemaphoreType.DMA
     vmem, hbm = pl.BlockSpec(memory_space=pltpu.VMEM), pl.BlockSpec(memory_space=pltpu.HBM)
     bred, factor = pl.pallas_call(
         functools.partial(kernel, nx_dev, ny_dev, members, rows, cols),
         out_shape=(
-            jax.ShapeDtypeStruct((states, 3, 2, ext, 128), f32),
+            jax.ShapeDtypeStruct((members, 3, 2, rows, 128), f32),
             jax.ShapeDtypeStruct((members, 128), f32),
         ),
         in_specs=[hbm] * 2,
-        out_specs=[vmem] * 2,
+        out_specs=[hbm, vmem],
         scratch_shapes=[
             pltpu.VMEM((states, 3, ext, cols), f32),
             pltpu.VMEM((2, 2, 3, rows, 128), f32),
             pltpu.VMEM((2, 2, 3, ext, 128), f32),
-            pltpu.VMEM((2, 3, 2, ext, 128), f32),
             pltpu.VMEM((256, 128), jnp.bfloat16),
-            pltpu.VMEM((4, 5, tall + 4, 8, 128), f32),
-            pltpu.VMEM((4, 5, tall + 4, 8, 128), f32),
-            pltpu.VMEM((3, 5, tall, 8, 128), f32),
-            pltpu.VMEM((3, 5, tall, 8, 128), f32),
-            pltpu.VMEM((tall, 8, 128), f32),
+            pltpu.VMEM((4, 5, ext, 128), f32),
+            pltpu.VMEM((4, 5, ext, 128), f32),
+            pltpu.VMEM((3, 5, ext, 128), f32),
+            pltpu.VMEM((3, 5, rows, 128), f32),
+            pltpu.VMEM((ext, 128), f32),
+            pltpu.VMEM((states, 3, 2, rows, 128), f32),
             pltpu.VMEM((members, members, 8, 128), f32),
             pltpu.VMEM((nx_dev, 8, 128), f32),
             pltpu.VMEM((ny_dev, 8, 128), f32),
             dma((members // 4 + 1,)),
+            dma((members // 2 + 1,)),
             dma((2, members // 2 + 1)),
             dma((2, members // 2 + 1)),
             dma((2, 3)),
@@ -370,25 +372,27 @@
             dma((ny_dev,)),
         ],
         compiler_params=pltpu.CompilerParams(
-            collective_id=0, has_side_effects=True, vmem_limit_bytes=24 * 1024 * 1024
+            collective_id=0, has_side_effects=True, vmem_limit_bytes=60 * 1024 * 1024
         ),
     )(control, perts)
     length = float(3 * rows * ny_dev * cols * nx_dev)
     return pl.pallas_call(
-        functools.partial(apply_kernel, length, members, rows),
+        functools.partial(apply_kernel, length, members),
         out_shape=(
             jax.ShapeDtypeStruct(perts.shape, f32),
             jax.ShapeDtypeStruct((members, members), f32),
         ),
-        in_specs=[vmem] * 2,
+        in_specs=[hbm] * 2,
         out_specs=[hbm] * 2,
         scratch_shapes=[
+            pltpu.VMEM((members, 3, 2, rows, 128), f32),
+            pltpu.VMEM((members, 128), f32),
             pltpu.VMEM((members, members, 128), f32),
             pltpu.VMEM((members, 3, rows, cols), f32),
             pltpu.VMEM((members, members), f32),
-            dma((4,)),
+            dma((8,)),
         ],
-        compiler_params=pltpu.CompilerParams(vmem_limit_bytes=24 * 1024 * 1024),
+        compiler_params=pltpu.CompilerParams(vmem_limit_bytes=60 * 1024 * 1024),
     )(bred, factor)
 
 

time: 44.3 us -> 41.2 us (0.930)
  local copies, waits for them, and re-layouts: 2.29 us -> 0 us
  Pallas kernels: 41.2 us -> 40.4 us
    unnamed x4 -> x0, local copies, waits for them, and re-layouts: 2.29 us -> none
    pallas_call x1, Pallas kernels: 39.4 us -> 37.6 us  [body(): pl.pallas_call(functools.partial(kernel, nx_dev, ny_dev, members, rows, c...]
    pallas_call x1, Pallas kernels: 1.81 us -> 2.78 us  [body(): pl.pallas_call(functools.partial(apply_kernel, length, members), out_shap...]
where the time goes in v3:
time: 41.2 us; the launch traced here: 41 us
  Pallas kernels  40.4 us (98%)
  between operations  0.64 us (2%)
    pallas_call x1, Pallas kernels, body(): pl.pallas_call(functools.partial(kernel, nx_dev, ny_dev, members, rows, c...  37.6 us
    pallas_call x1, Pallas kernels, body(): pl.pallas_call(functools.partial(apply_kernel, length, members), out_shap...  2.78 us

profile of v3, /device:TPU:1, one launch (start us, length us, event | category | flops | bytes accessed | tf_op | source)
XLA Modules:
  0.0 41.0 jit_solution(6983708739634275425)
XLA Ops:
  0.6 37.6 %shard_map.41 = (f32[16,3,2,32,128]{4,3,2,1,0:T(8,128)}, f32[16,128]{1,0:T(8,128)}) custom-call(f32[3,32,256]{2,1,0:T(8,128)} %ctrl_hbm.1, f32[16,3,32,256]{3,2,1,0:T(8,128)} %perts_hbm.1), custom_call_target="tpu_custom_call" | custom-call | tf_op jit(solution)/shard_map/pallas_call | solution.py:341
  38.2 2.8 %shard_map.42 = (f32[16,3,32,256]{3,2,1,0:T(8,128)}, f32[16,16]{1,0:T(8,128)}) custom-call(f32[16,3,2,32,128]{4,3,2,1,0:T(8,128)} %get-tuple-element.4.bred_hbm, f32[16,128]{1,0:T(8,128)} %get-tuple-element.5.factor_hbm), custom_call_target="tpu_custom_call" | custom-call | tf_op jit(solution)/shard_map/pallas_call | solution.py:379

commit v4 on v3

--- a/solution.py
+++ b/solution.py
@@ -11,6 +11,8 @@
 MESH = pl.DeviceIdType.MESH
 HALO = 8
 STEPS = 2
+ALL_RINGS, CONTROL_RINGS = (0, 1, 2, 3, 4), (0, 1, 4)
+SAME_RING = ((0, 2), (1, 3), (4,))
 MEAN_DEPTH = 4.0
 TIME_STEP = 0.1
 SCALE = TIME_STEP * (2.0 / 3.0)
@@ -19,7 +21,7 @@
 def kernel(
     nx_dev, ny_dev, members, rows, cols,
     ctrl_hbm, perts_hbm, bred_hbm, factor_ref,
-    st, pk, halo, band, now, mid, cini, cfin, cor, fin, parts, red1, red2,
+    st, pk, halo, band, stages, last, cini, cfin, cor, fin, parts, red1, red2,
     in_sem, out_sem, y_send, y_recv, x_send, x_recv, r1_send, r1_recv, r2_send, r2_recv,
 ):
     gx, gy = lax.axis_index("gx"), lax.axis_index("gy")
@@ -51,9 +53,6 @@
     row = gy * rows - HALO + grid_rows + lax.broadcasted_iota(jnp.int32, (ext, 128), 0)
     row = lax.rem(row, grid_rows).astype(jnp.float32)
     cor[...] = TIME_STEP * 0.5 * (1.0 + 0.5 * jnp.sin(2.0 * math.pi * row / float(grid_rows)))
-    for f in range(3):
-        cini[f] = jnp.full(cini.shape[1:], SCALE * SCALE * MEAN_DEPTH if f == 0 else 0.0, jnp.float32)
-    cfin[...] = jnp.zeros_like(cfin)
 
     for k in range(members // 4 + 1):
         own_copy(k).wait()
@@ -75,24 +74,22 @@
         pk[0, 1, f] = st[0, f, HALO : HALO + rows, 0:128]
         pk[1, 1, f] = st[0, f, HALO : HALO + rows, cols - 128 : cols]
 
-    def x_copies():
-        out = []
-        for side, x_to in ((0, left), (1, right)):
-            for place, (start, count, to, y_to) in enumerate(
-                ((0, rows, HALO, gy), (0, HALO, HALO + rows, up), (rows - HALO, HALO, 0, down))
-            ):
-                out.append(
-                    pltpu.make_async_remote_copy(
-                        pk.at[side, :, :, pl.ds(start, count), :],
-                        halo.at[side, :, :, pl.ds(to, count), :],
-                        x_send.at[side, place], x_recv.at[side, place],
-                        device_id=(x_to, y_to), device_id_type=MESH)
-                )
-        return out
-
+    def x_copies(place, tile):
+        start, count, to, y_to = ((0, rows, HALO, gy), (0, HALO, HALO + rows, up), (rows - HALO, HALO, 0, down))[place]
+        return [
+            pltpu.make_async_remote_copy(
+                pk.at[side, tile, :, pl.ds(start, count), :],
+                halo.at[side, tile, :, pl.ds(to, count), :],
+                x_send.at[side, place, tile], x_recv.at[side, place, tile],
+                device_id=(x_to, y_to), device_id_type=MESH)
+            for side, x_to in ((0, left), (1, right))
+        ]
+
+    everything = [(place, tile) for place in range(3) for tile in (1, 0)]
     pl.semaphore_wait(barrier, len(greeted))
-    for copy in x_copies():
-        copy.start()
+    for key in everything:
+        for copy in x_copies(*key):
+            copy.start()
 
     def y_copies(p, field_ref, st_ref):
         lead = (slice(None),) * (len(field_ref.shape) - 2)
@@ -118,114 +115,145 @@
         for copy in pair_y(p):
             copy.start()
 
-    for copy in x_copies():
-        copy.wait_recv()
-
     k_id = lax.rem(lax.broadcasted_iota(jnp.int32, (256, 128), 0), 128)
     ahead = lax.rem(k_id - lax.broadcasted_iota(jnp.int32, (256, 128), 1) + 128, 128)
     weights = jnp.where(ahead == 1, 1.0, jnp.where(ahead == 127, -1.0, 0.0))
     weights = jnp.where(ahead == 2, -0.125, jnp.where(ahead == 126, 0.125, weights))
     band[...] = weights.astype(jnp.bfloat16)
 
-    def put_state(ref, i, at, h, e, n):
-        for f, z in enumerate((h, e, n, h * n)):
-            ref[f, i, at : at + 8] = z
-
-    def slopes_x(ref, i, starts):
-        h, e, n = ([ref[f, i, at : at + 8] for at in starts] for f in range(3))
-        z = jnp.concatenate(h + e + n + [u * v for u, v in zip(h, e)], axis=0)
-        top = z.astype(jnp.bfloat16)
-        rest = (z - top.astype(jnp.float32)).astype(jnp.bfloat16)
-        out = jnp.dot(jnp.concatenate([top, rest], axis=1), band[...], preferred_element_type=jnp.float32)
-        return out.reshape(4, len(starts), 8, 128)
-
-    def slope_y(ref, f, i, at):
-        z = [ref[f, i, at + d : at + d + 8] for d in (-2, -1, 1, 2)]
-        return (z[2] - z[1]) - 0.125 * (z[3] - z[0])
-
-    def forward(ref, i, at, along):
-        h, e, n = (ref[f, i, at : at + 8] for f in range(3))
-        c = cor[at : at + 8]
-        new_h = h - along[3] - slope_y(ref, 3, i, at)
-        new_e = e - (e * along[1] + n * (slope_y(ref, 1, i, at) - c) + along[0])
-        new_n = n - (e * (along[2] + c) + n * slope_y(ref, 2, i, at) + slope_y(ref, 0, i, at))
-        return new_h, new_e, new_n
-
-    def bred_out(p):
-        return pltpu.make_async_copy(fin.at[pl.ds(2 * p - 1, 2)], bred_hbm.at[pl.ds(2 * p - 2, 2)], out_sem.at[p])
-
-    inner = [list(range(2 * w, ext - 2 * w - 7, 8)) for w in (1, 2, 2, 4)]
-    inner[0].append(ext - 10)
-
-    @pl.loop(0, pairs)
-    def _(p):
-        @pl.when(p == 0)
-        def _():
-            for copy in control_y():
-                copy.wait_recv()
-
-        @pl.when(p > 0)
-        def _():
-            for copy in pair_y(p):
-                copy.wait_recv()
-
-        slot = jnp.where(p == 0, 1, 0)
-        first = jnp.maximum(2 * p - 1, 0)
-        places = (jnp.maximum(first - 1, 0), jnp.maximum(2 * p - 1, 0))
-        for f in range(3):
-            scale = SCALE * SCALE if f == 0 else SCALE
-            for at in range(0, ext, 8):
-                pick = slice(at, at + 8)
+    def assemble(p, starts):
+        control = isinstance(p, int)
+        slot, states = (1, (0, 0)) if control else (0, (2 * p - 1, 2 * p))
+        for at in starts:
+            pick = slice(at, at + 8)
+            state = []
+            for f in range(3):
                 after, before = halo[0, slot, f, pick, :], halo[1, slot, f, pick, :]
                 rings, middle = [], []
-                for k, m in zip((first, 2 * p), places):
+                for k in states:
                     low, high = st[k, f, pick, 0:128], st[k, f, pick, 128:256]
-                    beyond = pltpu.roll(jnp.where(lane // 8 == m, after, before), lax.rem(128 - 8 * m, 128), 1)
+                    if control:
+                        beyond = jnp.where(lane < 8, after, before)
+                    else:
+                        beyond = pltpu.roll(jnp.where(lane // 8 == k - 1, after, before), lax.rem(136 - 8 * k, 128), 1)
                     rings.append(jnp.where(lane < 120, low, beyond))
                     rings.append(jnp.where(lane < 8, beyond, high))
                     middle.append(jnp.where(lane < 64, high, low))
                 apart = pltpu.roll(middle[1], 64, 1)
                 rings.append(jnp.where((lane < 32) | (lane >= 96), middle[0], apart))
-                for i in range(5):
-                    now[f, i, pick] = cini[f, i, pick] + scale * rings[i]
-
-        @pl.when(p == 0)
-        def _():
-            cini[...] = now[:3]
-
-        for i in range(5):
-            for at in range(0, ext, 8):
-                now[3, i, at : at + 8] = now[0, i, at : at + 8] * now[2, i, at : at + 8]
-
-        for step in range(STEPS):
-            for i in range(5):
-                starts = inner[2 * step]
-                along = slopes_x(now, i, starts)
-                for j, at in enumerate(starts):
-                    put_state(mid, i, at, *forward(now, i, at, along[:, j]))
-            for i in range(5):
-                starts = inner[2 * step + 1]
-                along = slopes_x(mid, i, starts)
-                for j, at in enumerate(starts):
-                    new = forward(mid, i, at, along[:, j])
-                    put_state(now, i, at, *(0.5 * (now[f, i, at : at + 8] + new[f]) for f in range(3)))
-
+                scale = SCALE * SCALE if f == 0 else SCALE
+                if control:
+                    rings = [scale * z + (scale * MEAN_DEPTH if f == 0 else 0.0) for z in rings]
+                    for same in SAME_RING:
+                        for i in same:
+                            cini[f, i, pick] = rings[same[0]]
+                else:
+                    rings = [cini[f, i, pick] + scale * z for i, z in enumerate(rings)]
+                state.append(rings)
+            for i in CONTROL_RINGS if control else ALL_RINGS:
+                put_state(p, 0, i, at, *(state[f][i] for f in range(3)))
+
+    def put_state(p, stage, i, at, h, e, n):
+        for f, z in enumerate((h, e, n, h * n)):
+            stages[stage, p, f, i, at : at + 8] = z
+
+    def slopes_x(p, stage, units):
+        h, e, n = ([stages[stage, p, f, i, at : at + 8] for i, at in units] for f in range(3))
+        z = jnp.concatenate(h + e + n + [u * v for u, v in zip(h, e)], axis=0)
+        top = z.astype(jnp.bfloat16)
+        rest = (z - top.astype(jnp.float32)).astype(jnp.bfloat16)
+        out = jnp.dot(jnp.concatenate([top, rest], axis=1), band[...], preferred_element_type=jnp.float32)
+        return out.reshape(4, len(units), 8, 128)
+
+    def slope_y(p, stage, f, i, at):
+        z = [stages[stage, p, f, i, at + d : at + d + 8] for d in (-2, -1, 1, 2)]
+        return (z[2] - z[1]) - 0.125 * (z[3] - z[0])
+
+    def forward(p, stage, i, at, along):
+        h, e, n = (stages[stage, p, f, i, at : at + 8] for f in range(3))
+        c = cor[at : at + 8]
+        new_h = h - along[3] - slope_y(p, stage, 3, i, at)
+        new_e = e - (e * along[1] + n * (slope_y(p, stage, 1, i, at) - c) + along[0])
+        new_n = n - (e * (along[2] + c) + n * slope_y(p, stage, 2, i, at) + slope_y(p, stage, 0, i, at))
+        return new_h, new_e, new_n
+
+    def evaluate(p, stage, units, u=0):
+        along = slopes_x(p, stage, units)
+        for j, (i, at) in enumerate(units):
+            new = forward(p, stage, i, at, along[:, j])
+            if stage % 2 == 1:
+                new = [0.5 * (stages[stage - 1, p, f, i, at : at + 8] + new[f]) for f in range(3)]
+            if stage < 2 * STEPS - 1:
+                put_state(p, stage + 1, i, at, *new)
+            else:
+                for f in range(3):
+                    last[u, f, i, at - HALO : at - HALO + 8] = new[f]
+
+    def finish(p, starts, u=0):
         for f in range(3):
             scale = 1.0 / (SCALE * SCALE) if f == 0 else 1.0 / SCALE
-            for at in range(0, rows, 8):
-                pick, to = slice(HALO + at, HALO + at + 8), slice(at, at + 8)
-                z = [scale * (now[f, i, pick] - cfin[f, i, to]) for i in range(5)]
-                for s, k in enumerate((first, 2 * p)):
+            for at in starts:
+                to = slice(at - HALO, at - HALO + 8)
+                if isinstance(p, int):
+                    for same in SAME_RING:
+                        for i in same:
+                            cfin[f, i, to] = last[u, f, same[0], to]
+                    continue
+                z = [scale * (last[u, f, i, to] - cfin[f, i, to]) for i in ALL_RINGS]
+                for s, k in enumerate((2 * p - 1, 2 * p)):
                     both = z[4] if s == 0 else pltpu.roll(z[4], 64, 1)
                     fin[k, f, 0, to, :] = jnp.where(lane < 112, z[2 * s], both)
                     fin[k, f, 1, to, :] = jnp.where(lane < 16, both, z[2 * s + 1])
 
-        @pl.when(p == 0)
-        def _():
-            cfin[...] = now[:3, :, HALO : HALO + rows]
-
-        @pl.when(p > 0)
-        def _():
+    def inner(chosen):
+        for p in chosen:
+            assemble(p, range(HALO, HALO + rows, 8))
+        for stage in range(2 * STEPS):
+            low, high = HALO + 2 * stage + 2, HALO + rows - 2 * stage - 2
+            starts = [min(at, high - 8) for at in range(low, high, 8)]
+            for u, p in enumerate(chosen):
+                for i in CONTROL_RINGS if isinstance(p, int) else ALL_RINGS:
+                    evaluate(p, stage, [(i, at) for at in starts], u)
+        for u, p in enumerate(chosen):
+            finish(p, starts, u)
+
+    def edges(chosen):
+        for p in chosen:
+            assemble(p, (0, HALO + rows))
+        for stage in range(2 * STEPS):
+            starts = (2 * stage + 2, rows + 2 * HALO - 2 * stage - 10)
+            for u, p in enumerate(chosen):
+                for i in CONTROL_RINGS if isinstance(p, int) else ALL_RINGS:
+                    evaluate(p, stage, [(i, at) for at in starts], u)
+        for u, p in enumerate(chosen):
+            finish(p, starts, u)
+
+    def bred_out(p):
+        return pltpu.make_async_copy(fin.at[pl.ds(2 * p - 1, 2)], bred_hbm.at[pl.ds(2 * p - 2, 2)], out_sem.at[p])
+
+    for copy in x_copies(0, 1):
+        copy.wait_recv()
+    inner([0])
+    for copy in x_copies(0, 0):
+        copy.wait_recv()
+
+    @pl.loop(0, members // 4)
+    def _(q):
+        inner([2 * q + 1, 2 * q + 2])
+
+    for copy in x_copies(1, 1) + x_copies(2, 1) + control_y():
+        copy.wait_recv()
+    edges([0])
+    for copy in x_copies(1, 0) + x_copies(2, 0):
+        copy.wait_recv()
+
+    @pl.loop(0, members // 4)
+    def _(q):
+        for p in (2 * q + 1, 2 * q + 2):
+            for copy in pair_y(p):
+                copy.wait_recv()
+        edges([2 * q + 1, 2 * q + 2])
+        for p in (2 * q + 1, 2 * q + 2):
             bred_out(p).start()
 
     @pl.loop(0, members // 4)
@@ -280,7 +308,7 @@
     def _(p):
         bred_out(p).wait()
 
-    for copy in x_copies() + control_y():
+    for copy in [copy for key in everything for copy in x_copies(*key)] + control_y():
         copy.wait_send()
 
     @pl.loop(1, pairs)
@@ -301,32 +329,37 @@
 
 
 def apply_kernel(length, members, bred_hbm, factor_hbm, basis_hbm, rfac_hbm, bred, factor, table, out, rout, sem):
-    first = pltpu.make_async_copy(factor_hbm, factor, sem.at[4])
+    first = pltpu.make_async_copy(factor_hbm, factor, sem.at[7])
     first.start()
-    parts = [pltpu.make_async_copy(bred_hbm.at[:, pl.ds(f, 1)], bred.at[:, pl.ds(f, 1)], sem.at[5 + f]) for f in range(3)]
+    parts = [
+        pltpu.make_async_copy(bred_hbm.at[:, pl.ds(f, 1), pl.ds(i, 1)], bred.at[:, pl.ds(f, 1), pl.ds(i, 1)], sem.at[8 + 2 * f + i])
+        for f in range(3)
+        for i in range(2)
+    ]
     for copy in parts:
         copy.start()
     first.wait()
     row_id = lax.broadcasted_iota(jnp.int32, (members, members), 0)
     col_id = lax.broadcasted_iota(jnp.int32, (members, members), 1)
     rout[...] = jnp.where(row_id <= col_id, factor[:, :members] * (1.0 / math.sqrt(length)), 0.0)
-    small = pltpu.make_async_copy(rout, rfac_hbm, sem.at[3])
+    small = pltpu.make_async_copy(rout, rfac_hbm, sem.at[6])
     small.start()
     for j in range(members):
         column = factor[:, members + j : members + j + 1] * math.sqrt(length)
         table[j] = jnp.broadcast_to(column, (members, 128))
     copies = []
     for f in range(3):
-        parts[f].wait()
         for i in range(2):
+            parts[2 * f + i].wait()
             x = [bred[j, f, i] for j in range(members)]
             for m in range(members):
                 total = table[0, m : m + 1, :] * x[0]
                 for j in range(1, m + 1):
                     total = total + table[j, m : m + 1, :] * x[j]
                 out[m, f, :, 128 * i : 128 * (i + 1)] = total
-        copies.append(pltpu.make_async_copy(out.at[:, pl.ds(f, 1)], basis_hbm.at[:, pl.ds(f, 1)], sem.at[f]))
-        copies[-1].start()
+            half = (slice(None), pl.ds(f, 1), slice(None), pl.ds(128 * i, 128))
+            copies.append(pltpu.make_async_copy(out.at[half], basis_hbm.at[half], sem.at[2 * f + i]))
+            copies[-1].start()
     for copy in copies + [small]:
         copy.wait()
 
@@ -351,8 +384,8 @@
             pltpu.VMEM((2, 2, 3, rows, 128), f32),
             pltpu.VMEM((2, 2, 3, ext, 128), f32),
             pltpu.VMEM((256, 128), jnp.bfloat16),
-            pltpu.VMEM((4, 5, ext, 128), f32),
-            pltpu.VMEM((4, 5, ext, 128), f32),
+            pltpu.VMEM((2 * STEPS, members // 2 + 1, 4, 5, ext, 128), f32),
+            pltpu.VMEM((2, 3, 5, rows, 128), f32),
             pltpu.VMEM((3, 5, ext, 128), f32),
             pltpu.VMEM((3, 5, rows, 128), f32),
             pltpu.VMEM((ext, 128), f32),
@@ -364,8 +397,8 @@
             dma((members // 2 + 1,)),
             dma((2, members // 2 + 1)),
             dma((2, members // 2 + 1)),
-            dma((2, 3)),
-            dma((2, 3)),
+            dma((2, 3, 2)),
+            dma((2, 3, 2)),
             dma((nx_dev,)),
             dma((nx_dev,)),
             dma((ny_dev,)),
@@ -390,7 +423,7 @@
             pltpu.VMEM((members, members, 128), f32),
             pltpu.VMEM((members, 3, rows, cols), f32),
             pltpu.VMEM((members, members), f32),
-            dma((8,)),
+            dma((14,)),
         ],
         compiler_params=pltpu.CompilerParams(vmem_limit_bytes=60 * 1024 * 1024),
     )(bred, factor)

time: 41.2 us -> 39.8 us (0.966)
  Pallas kernels: 40.4 us -> 39 us
    pallas_call x1, Pallas kernels: 37.6 us -> 36.3 us  [body(): pl.pallas_call(functools.partial(kernel, nx_dev, ny_dev, members, rows, c...]
where the time goes in v4:
time: 39.8 us; the launch traced here: 39.6 us
  Pallas kernels  39 us (98%)
  between operations  0.64 us (2%)
    pallas_call x1, Pallas kernels, body(): pl.pallas_call(functools.partial(kernel, nx_dev, ny_dev, members, rows, c...  36.3 us
    pallas_call x1, Pallas kernels, body(): pl.pallas_call(functools.partial(apply_kernel, length, members), out_shap...  2.67 us

profile of v4, /device:TPU:1, one launch (start us, length us, event | category | flops | bytes accessed | tf_op | source)
XLA Modules:
  0.0 39.6 jit_solution(13491166334353611371)
XLA Ops:
  0.6 36.3 %shard_map.41 = (f32[16,3,2,32,128]{4,3,2,1,0:T(8,128)}, f32[16,128]{1,0:T(8,128)}) custom-call(f32[3,32,256]{2,1,0:T(8,128)} %ctrl_hbm.1, f32[16,3,32,256]{3,2,1,0:T(8,128)} %perts_hbm.1), custom_call_target="tpu_custom_call" | custom-call | tf_op jit(solution)/shard_map/pallas_call | solution.py:374
  36.9 2.7 %shard_map.42 = (f32[16,3,32,256]{3,2,1,0:T(8,128)}, f32[16,16]{1,0:T(8,128)}) custom-call(f32[16,3,2,32,128]{4,3,2,1,0:T(8,128)} %get-tuple-element.4.bred_hbm, f32[16,128]{1,0:T(8,128)} %get-tuple-element.5.factor_hbm), custom_call_target="tpu_custom_call" | custom-call | tf_op jit(solution)/shard_map/pallas_call | solution.py:412

commit v5 on v4

--- a/solution.py
+++ b/solution.py
@@ -11,7 +11,7 @@
 MESH = pl.DeviceIdType.MESH
 HALO = 8
 STEPS = 2
-ALL_RINGS, CONTROL_RINGS = (0, 1, 2, 3, 4), (0, 1, 4)
+ALL_RINGS, OUTER_RINGS, MIDDLE_RING = (0, 1, 2, 3, 4), (0, 1, 2, 3), (4,)
 SAME_RING = ((0, 2), (1, 3), (4,))
 MEAN_DEPTH = 4.0
 TIME_STEP = 0.1
@@ -110,7 +110,7 @@
     for copy in control_y():
         copy.start()
 
-    @pl.loop(1, pairs)
+    @pl.loop(1, 5)
     def _(p):
         for copy in pair_y(p):
             copy.start()
@@ -121,36 +121,41 @@
     weights = jnp.where(ahead == 2, -0.125, jnp.where(ahead == 126, 0.125, weights))
     band[...] = weights.astype(jnp.bfloat16)
 
-    def assemble(p, starts):
+    def of_control(p, rings):
+        return [i for i in rings if i in (0, 1, 4)] if isinstance(p, int) else rings
+
+    def assemble(p, starts, rings):
         control = isinstance(p, int)
         slot, states = (1, (0, 0)) if control else (0, (2 * p - 1, 2 * p))
         for at in starts:
             pick = slice(at, at + 8)
             state = []
             for f in range(3):
-                after, before = halo[0, slot, f, pick, :], halo[1, slot, f, pick, :]
-                rings, middle = [], []
-                for k in states:
-                    low, high = st[k, f, pick, 0:128], st[k, f, pick, 128:256]
-                    if control:
-                        beyond = jnp.where(lane < 8, after, before)
-                    else:
-                        beyond = pltpu.roll(jnp.where(lane // 8 == k - 1, after, before), lax.rem(136 - 8 * k, 128), 1)
-                    rings.append(jnp.where(lane < 120, low, beyond))
-                    rings.append(jnp.where(lane < 8, beyond, high))
-                    middle.append(jnp.where(lane < 64, high, low))
-                apart = pltpu.roll(middle[1], 64, 1)
-                rings.append(jnp.where((lane < 32) | (lane >= 96), middle[0], apart))
+                tiles = [[st[k, f, pick, 128 * i : 128 * (i + 1)] for i in range(2)] for k in states]
+                full = {}
+                if 0 in rings:
+                    after, before = halo[0, slot, f, pick, :], halo[1, slot, f, pick, :]
+                    for s, k in enumerate(states):
+                        if control:
+                            beyond = jnp.where(lane < 8, after, before)
+                        else:
+                            beyond = pltpu.roll(jnp.where(lane // 8 == k - 1, after, before), lax.rem(136 - 8 * k, 128), 1)
+                        full[2 * s] = jnp.where(lane < 120, tiles[s][0], beyond)
+                        full[2 * s + 1] = jnp.where(lane < 8, beyond, tiles[s][1])
+                if 4 in rings:
+                    middle = [jnp.where(lane < 64, high, low) for low, high in tiles]
+                    full[4] = jnp.where((lane < 32) | (lane >= 96), middle[0], pltpu.roll(middle[1], 64, 1))
                 scale = SCALE * SCALE if f == 0 else SCALE
                 if control:
-                    rings = [scale * z + (scale * MEAN_DEPTH if f == 0 else 0.0) for z in rings]
+                    full = {i: scale * z + (scale * MEAN_DEPTH if f == 0 else 0.0) for i, z in full.items()}
                     for same in SAME_RING:
-                        for i in same:
-                            cini[f, i, pick] = rings[same[0]]
+                        if same[0] in full:
+                            for i in same:
+                                cini[f, i, pick] = full[same[0]]
                 else:
-                    rings = [cini[f, i, pick] + scale * z for i, z in enumerate(rings)]
-                state.append(rings)
-            for i in CONTROL_RINGS if control else ALL_RINGS:
+                    full = {i: cini[f, i, pick] + scale * z for i, z in full.items()}
+                state.append(full)
+            for i in of_control(p, rings):
                 put_state(p, 0, i, at, *(state[f][i] for f in range(3)))
 
     def put_state(p, stage, i, at, h, e, n):
@@ -177,7 +182,7 @@
         new_n = n - (e * (along[2] + c) + n * slope_y(p, stage, 2, i, at) + slope_y(p, stage, 0, i, at))
         return new_h, new_e, new_n
 
-    def evaluate(p, stage, units, u=0):
+    def evaluate(p, stage, units):
         along = slopes_x(p, stage, units)
         for j, (i, at) in enumerate(units):
             new = forward(p, stage, i, at, along[:, j])
@@ -187,9 +192,9 @@
                 put_state(p, stage + 1, i, at, *new)
             else:
                 for f in range(3):
-                    last[u, f, i, at - HALO : at - HALO + 8] = new[f]
-
-    def finish(p, starts, u=0):
+                    last[p, f, i, at - HALO : at - HALO + 8] = new[f]
+
+    def finish(p, starts):
         for f in range(3):
             scale = 1.0 / (SCALE * SCALE) if f == 0 else 1.0 / SCALE
             for at in starts:
@@ -197,49 +202,62 @@
                 if isinstance(p, int):
                     for same in SAME_RING:
                         for i in same:
-                            cfin[f, i, to] = last[u, f, same[0], to]
+                            cfin[f, i, to] = last[p, f, same[0], to]
                     continue
-                z = [scale * (last[u, f, i, to] - cfin[f, i, to]) for i in ALL_RINGS]
+                z = [scale * (last[p, f, i, to] - cfin[f, i, to]) for i in ALL_RINGS]
                 for s, k in enumerate((2 * p - 1, 2 * p)):
                     both = z[4] if s == 0 else pltpu.roll(z[4], 64, 1)
                     fin[k, f, 0, to, :] = jnp.where(lane < 112, z[2 * s], both)
                     fin[k, f, 1, to, :] = jnp.where(lane < 16, both, z[2 * s + 1])
 
-    def inner(chosen):
+    def inner(chosen, rings):
         for p in chosen:
-            assemble(p, range(HALO, HALO + rows, 8))
+            assemble(p, range(HALO, HALO + rows, 8), rings)
         for stage in range(2 * STEPS):
             low, high = HALO + 2 * stage + 2, HALO + rows - 2 * stage - 2
             starts = [min(at, high - 8) for at in range(low, high, 8)]
-            for u, p in enumerate(chosen):
-                for i in CONTROL_RINGS if isinstance(p, int) else ALL_RINGS:
-                    evaluate(p, stage, [(i, at) for at in starts], u)
-        for u, p in enumerate(chosen):
-            finish(p, starts, u)
+            for p in chosen:
+                for i in of_control(p, rings):
+                    evaluate(p, stage, [(i, at) for at in starts])
+        if 0 in rings:
+            for p in chosen:
+                finish(p, starts)
 
     def edges(chosen):
         for p in chosen:
-            assemble(p, (0, HALO + rows))
+            assemble(p, (0, HALO + rows), ALL_RINGS)
         for stage in range(2 * STEPS):
             starts = (2 * stage + 2, rows + 2 * HALO - 2 * stage - 10)
-            for u, p in enumerate(chosen):
-                for i in CONTROL_RINGS if isinstance(p, int) else ALL_RINGS:
-                    evaluate(p, stage, [(i, at) for at in starts], u)
-        for u, p in enumerate(chosen):
-            finish(p, starts, u)
+            for p in chosen:
+                for i in of_control(p, ALL_RINGS):
+                    evaluate(p, stage, [(i, at) for at in starts])
+        for p in chosen:
+            finish(p, starts)
 
     def bred_out(p):
         return pltpu.make_async_copy(fin.at[pl.ds(2 * p - 1, 2)], bred_hbm.at[pl.ds(2 * p - 2, 2)], out_sem.at[p])
 
+    inner([0], MIDDLE_RING)
+
+    @pl.loop(0, members // 8)
+    def _(q):
+        inner([4 * q + j for j in range(1, 5)], MIDDLE_RING)
+
     for copy in x_copies(0, 1):
         copy.wait_recv()
-    inner([0])
+    inner([0], OUTER_RINGS)
     for copy in x_copies(0, 0):
         copy.wait_recv()
 
     @pl.loop(0, members // 4)
     def _(q):
-        inner([2 * q + 1, 2 * q + 2])
+        @pl.when(q < members // 4 - 2)
+        def _():
+            for p in (2 * q + 5, 2 * q + 6):
+                for copy in pair_y(p):
+                    copy.start()
+
+        inner([2 * q + 1, 2 * q + 2], OUTER_RINGS)
 
     for copy in x_copies(1, 1) + x_copies(2, 1) + control_y():
         copy.wait_recv()
@@ -385,7 +403,7 @@
             pltpu.VMEM((2, 2, 3, ext, 128), f32),
             pltpu.VMEM((256, 128), jnp.bfloat16),
             pltpu.VMEM((2 * STEPS, members // 2 + 1, 4, 5, ext, 128), f32),
-            pltpu.VMEM((2, 3, 5, rows, 128), f32),
+            pltpu.VMEM((members // 2 + 1, 3, 5, rows, 128), f32),
             pltpu.VMEM((3, 5, ext, 128), f32),
             pltpu.VMEM((3, 5, rows, 128), f32),
             pltpu.VMEM((ext, 128), f32),

time: 39.8 us -> 39.8 us (level)
  no operation moved by 1% of the time
where the time goes in v5:
time: 39.8 us; the launch traced here: 39.6 us
  Pallas kernels  39 us (98%)
  between operations  0.64 us (2%)
    pallas_call x1, Pallas kernels, body(): pl.pallas_call(functools.partial(kernel, nx_dev, ny_dev, members, rows, c...  36.3 us
    pallas_call x1, Pallas kernels, body(): pl.pallas_call(functools.partial(apply_kernel, length, members), out_shap...  2.67 us

profile of v5, /device:TPU:1, one launch (start us, length us, event | category | flops | bytes accessed | tf_op | source)
XLA Modules:
  0.0 39.6 jit_solution(2248916538686024614)
XLA Ops:
  0.6 36.3 %shard_map.41 = (f32[16,3,2,32,128]{4,3,2,1,0:T(8,128)}, f32[16,128]{1,0:T(8,128)}) custom-call(f32[3,32,256]{2,1,0:T(8,128)} %ctrl_hbm.1, f32[16,3,32,256]{3,2,1,0:T(8,128)} %perts_hbm.1), custom_call_target="tpu_custom_call" | custom-call | tf_op jit(solution)/shard_map/pallas_call | solution.py:392
  36.9 2.7 %shard_map.42 = (f32[16,3,32,256]{3,2,1,0:T(8,128)}, f32[16,16]{1,0:T(8,128)}) custom-call(f32[16,3,2,32,128]{4,3,2,1,0:T(8,128)} %get-tuple-element.4.bred_hbm, f32[16,128]{1,0:T(8,128)} %get-tuple-element.5.factor_hbm), custom_call_target="tpu_custom_call" | custom-call | tf_op jit(solution)/shard_map/pallas_call | solution.py:430

commit v6 on v5

--- a/solution.py
+++ b/solution.py
@@ -21,7 +21,7 @@
 def kernel(
     nx_dev, ny_dev, members, rows, cols,
     ctrl_hbm, perts_hbm, bred_hbm, factor_ref,
-    st, pk, halo, band, stages, last, cini, cfin, cor, fin, parts, red1, red2,
+    st, pk, halo, pk1, halo1, band, stages, last, cini, cfin, cor, fin, parts, red1, red2,
     in_sem, out_sem, y_send, y_recv, x_send, x_recv, r1_send, r1_recv, r2_send, r2_recv,
 ):
     gx, gy = lax.axis_index("gx"), lax.axis_index("gy")
@@ -49,10 +49,31 @@
     for peer in greeted[8:]:
         pl.semaphore_signal(barrier, inc=1, device_id=peer, device_id_type=MESH)
 
-    grid_rows = rows * ny_dev
-    row = gy * rows - HALO + grid_rows + lax.broadcasted_iota(jnp.int32, (ext, 128), 0)
-    row = lax.rem(row, grid_rows).astype(jnp.float32)
-    cor[...] = TIME_STEP * 0.5 * (1.0 + 0.5 * jnp.sin(2.0 * math.pi * row / float(grid_rows)))
+    pl.semaphore_wait(barrier, len(greeted))
+
+    def y_copies(p, field_ref, st_ref):
+        lead = (slice(None),) * (len(field_ref.shape) - 2)
+        return [
+            pltpu.make_async_remote_copy(
+                field_ref.at[lead + (pl.ds(start, HALO),)],
+                st_ref.at[lead + (pl.ds(to, HALO),)],
+                y_send.at[way, p], y_recv.at[way, p], device_id=(gx, y_to), device_id_type=MESH)
+            for way, (start, to, y_to) in enumerate(((0, HALO + rows, up), (rows - HALO, 0, down)))
+        ]
+
+    def control_y():
+        return y_copies(0, ctrl_hbm, st.at[0])
+
+    def pair_y(p):
+        return y_copies(p, perts_hbm.at[pl.ds(2 * p - 2, 2)], st.at[pl.ds(2 * p - 1, 2)])
+
+    for copy in control_y():
+        copy.start()
+
+    @pl.loop(1, 3)
+    def _(p):
+        for copy in pair_y(p):
+            copy.start()
 
     for k in range(members // 4 + 1):
         own_copy(k).wait()
@@ -69,51 +90,42 @@
             both = pltpu.roll(jnp.where(wide < 8, head, tail), (8 * m) % 128, 1)
             first = jnp.where(wide == m, both, first)
             last = jnp.where(wide == (m + 15) % 16, both, last)
-        pk[0, 0, f] = first
-        pk[1, 0, f] = last
-        pk[0, 1, f] = st[0, f, HALO : HALO + rows, 0:128]
-        pk[1, 1, f] = st[0, f, HALO : HALO + rows, cols - 128 : cols]
+        pk[0, f] = first
+        pk[1, f] = last
+
+    for side in range(2):
+        both = jnp.zeros((rows, 128), jnp.float32)
+        for f in range(3):
+            tile = st[0, f, HALO : HALO + rows, 128 * side : 128 * (side + 1)]
+            both = jnp.where(wide == f, pltpu.roll(tile, 8 * (f + side), 1), both)
+        pk1[side] = both
 
     def x_copies(place, tile):
         start, count, to, y_to = ((0, rows, HALO, gy), (0, HALO, HALO + rows, up), (rows - HALO, HALO, 0, down))[place]
+        source, target, lead = ((pk, halo, (slice(None),)), (pk1, halo1, ()))[tile]
         return [
             pltpu.make_async_remote_copy(
-                pk.at[side, tile, :, pl.ds(start, count), :],
-                halo.at[side, tile, :, pl.ds(to, count), :],
+                source.at[(side,) + lead + (pl.ds(start, count),)],
+                target.at[(side,) + lead + (pl.ds(to, count),)],
                 x_send.at[side, place, tile], x_recv.at[side, place, tile],
                 device_id=(x_to, y_to), device_id_type=MESH)
             for side, x_to in ((0, left), (1, right))
         ]
 
     everything = [(place, tile) for place in range(3) for tile in (1, 0)]
-    pl.semaphore_wait(barrier, len(greeted))
     for key in everything:
         for copy in x_copies(*key):
             copy.start()
 
-    def y_copies(p, field_ref, st_ref):
-        lead = (slice(None),) * (len(field_ref.shape) - 2)
-        return [
-            pltpu.make_async_remote_copy(
-                field_ref.at[lead + (pl.ds(start, HALO),)],
-                st_ref.at[lead + (pl.ds(to, HALO),)],
-                y_send.at[way, p], y_recv.at[way, p], device_id=(gx, y_to), device_id_type=MESH)
-            for way, (start, to, y_to) in enumerate(((0, HALO + rows, up), (rows - HALO, 0, down)))
-        ]
-
-    def control_y():
-        return y_copies(0, ctrl_hbm, st.at[0])
-
-    def pair_y(p):
-        return y_copies(p, perts_hbm.at[pl.ds(2 * p - 2, 2)], st.at[pl.ds(2 * p - 1, 2)])
-
-    for copy in control_y():
-        copy.start()
-
-    @pl.loop(1, 5)
+    @pl.loop(3, pairs)
     def _(p):
         for copy in pair_y(p):
             copy.start()
+
+    grid_rows = rows * ny_dev
+    row = gy * rows - HALO + grid_rows + lax.broadcasted_iota(jnp.int32, (ext, 128), 0)
+    row = lax.rem(row, grid_rows).astype(jnp.float32)
+    cor[...] = TIME_STEP * 0.5 * (1.0 + 0.5 * jnp.sin(2.0 * math.pi * row / float(grid_rows)))
 
     k_id = lax.rem(lax.broadcasted_iota(jnp.int32, (256, 128), 0), 128)
     ahead = lax.rem(k_id - lax.broadcasted_iota(jnp.int32, (256, 128), 1) + 128, 128)
@@ -126,7 +138,7 @@
 
     def assemble(p, starts, rings):
         control = isinstance(p, int)
-        slot, states = (1, (0, 0)) if control else (0, (2 * p - 1, 2 * p))
+        states = (0, 0) if control else (2 * p - 1, 2 * p)
         for at in starts:
             pick = slice(at, at + 8)
             state = []
@@ -134,12 +146,13 @@
                 tiles = [[st[k, f, pick, 128 * i : 128 * (i + 1)] for i in range(2)] for k in states]
                 full = {}
                 if 0 in rings:
-                    after, before = halo[0, slot, f, pick, :], halo[1, slot, f, pick, :]
                     for s, k in enumerate(states):
                         if control:
-                            beyond = jnp.where(lane < 8, after, before)
+                            ends = (halo1[0, pick, :], halo1[1, pick, :])
+                            beyond = jnp.where(lane < 8, pltpu.roll(ends[0], (128 - 8 * f) % 128, 1), pltpu.roll(ends[1], 120 - 8 * f, 1))
                         else:
-                            beyond = pltpu.roll(jnp.where(lane // 8 == k - 1, after, before), lax.rem(136 - 8 * k, 128), 1)
+                            ends = (halo[0, f, pick, :], halo[1, f, pick, :])
+                            beyond = pltpu.roll(jnp.where(lane // 8 == k - 1, *ends), lax.rem(136 - 8 * k, 128), 1)
                         full[2 * s] = jnp.where(lane < 120, tiles[s][0], beyond)
                         full[2 * s + 1] = jnp.where(lane < 8, beyond, tiles[s][1])
                 if 4 in rings:
@@ -251,13 +264,32 @@
 
     @pl.loop(0, members // 4)
     def _(q):
-        @pl.when(q < members // 4 - 2)
-        def _():
-            for p in (2 * q + 5, 2 * q + 6):
-                for copy in pair_y(p):
-                    copy.start()
-
         inner([2 * q + 1, 2 * q + 2], OUTER_RINGS)
+
+    def products(a, b, cuts, fresh):
+        total = [[None] * 4 for _ in range(4)]
+        for f in range(3):
+            for i in range(2):
+                for cut in cuts:
+                    x = [fin[1 + 4 * a + u, f, i, cut] for u in range(4)]
+                    y = [fin[1 + 4 * b + u, f, i, cut] for u in range(4)]
+                    for u in range(4):
+                        for v in range(4):
+                            z = x[u] * y[v]
+                            total[u][v] = z if total[u][v] is None else total[u][v] + z
+        if not fresh:
+            total = [[parts[4 * a + u, 4 * b + v] + total[u][v] for v in range(4)] for u in range(4)]
+        for u in range(4):
+            for v in range(4):
+                parts[4 * a + u, 4 * b + v] = total[u][v]
+                if not fresh:
+                    parts[4 * b + v, 4 * a + u] = total[u][v]
+
+    @pl.loop(0, members // 4)
+    def _(a):
+        @pl.loop(0, a + 1)
+        def _(b):
+            products(a, b, [slice(at, at + 8) for at in range(8, rows - 8, 8)], True)
 
     for copy in x_copies(1, 1) + x_copies(2, 1) + control_y():
         copy.wait_recv()
@@ -265,32 +297,18 @@
     for copy in x_copies(1, 0) + x_copies(2, 0):
         copy.wait_recv()
 
-    @pl.loop(0, members // 4)
-    def _(q):
-        for p in (2 * q + 1, 2 * q + 2):
-            for copy in pair_y(p):
-                copy.wait_recv()
-        edges([2 * q + 1, 2 * q + 2])
-        for p in (2 * q + 1, 2 * q + 2):
-            bred_out(p).start()
-
-    @pl.loop(0, members // 4)
-    def _(a):
-        @pl.loop(0, a + 1)
-        def _(b):
-            total = [[None] * 4 for _ in range(4)]
-            for f in range(3):
-                for i in range(2):
-                    x = [fin[1 + 4 * a + u, f, i] for u in range(4)]
-                    y = [fin[1 + 4 * b + u, f, i] for u in range(4)]
-                    for u in range(4):
-                        for v in range(4):
-                            z = jnp.sum((x[u] * y[v]).reshape(rows // 8, 8, 128), axis=0)
-                            total[u][v] = z if total[u][v] is None else total[u][v] + z
-            for u in range(4):
-                for v in range(4):
-                    parts[4 * a + u, 4 * b + v] = total[u][v]
-                    parts[4 * b + v, 4 * a + u] = total[u][v]
+    @pl.loop(1, pairs)
+    def _(p):
+        for copy in pair_y(p):
+            copy.wait_recv()
+        edges([p])
+        bred_out(p).start()
+
+        @pl.when(p % 2 == 0)
+        def _():
+            @pl.loop(0, p // 2)
+            def _(b):
+                products(p // 2 - 1, b, [slice(0, 8), slice(rows - 8, rows)], False)
 
     row_id = lax.broadcasted_iota(jnp.int32, (members, 128), 0)
     col_id = lax.broadcasted_iota(jnp.int32, (members, 128), 1)
@@ -399,8 +417,10 @@
         out_specs=[hbm, vmem],
         scratch_shapes=[
             pltpu.VMEM((states, 3, ext, cols), f32),
-            pltpu.VMEM((2, 2, 3, rows, 128), f32),
-            pltpu.VMEM((2, 2, 3, ext, 128), f32),
+            pltpu.VMEM((2, 3, rows, 128), f32),
+            pltpu.VMEM((2, 3, ext, 128), f32),
+            pltpu.VMEM((2, rows, 128), f32),
+            pltpu.VMEM((2, ext, 128), f32),
             pltpu.VMEM((256, 128), jnp.bfloat16),
             pltpu.VMEM((2 * STEPS, members // 2 + 1, 4, 5, ext, 128), f32),
             pltpu.VMEM((members // 2 + 1, 3, 5, rows, 128), f32),

time: 39.8 us -> 39.8 us (level)
  no operation moved by 1% of the time
where the time goes in v6:
time: 39.8 us; the launch traced here: 39.7 us
  Pallas kernels  39.1 us (98%)
  between operations  0.64 us (2%)
    pallas_call x1, Pallas kernels, body(): pl.pallas_call(functools.partial(kernel, nx_dev, ny_dev, members, rows, c...  36.4 us
    pallas_call x1, Pallas kernels, body(): pl.pallas_call(functools.partial(apply_kernel, length, members), out_shap...  2.67 us

profile of v6, /device:TPU:1, one launch (start us, length us, event | category | flops | bytes accessed | tf_op | source)
XLA Modules:
  0.0 39.7 jit_solution(5778914560098899480)
XLA Ops:
  0.6 36.4 %shard_map.41 = (f32[16,3,2,32,128]{4,3,2,1,0:T(8,128)}, f32[16,128]{1,0:T(8,128)}) custom-call(f32[3,32,256]{2,1,0:T(8,128)} %ctrl_hbm.1, f32[16,3,32,256]{3,2,1,0:T(8,128)} %perts_hbm.1), custom_call_target="tpu_custom_call" | custom-call | tf_op jit(solution)/shard_map/pallas_call | solution.py:410
  37.0 2.7 %shard_map.42 = (f32[16,3,32,256]{3,2,1,0:T(8,128)}, f32[16,16]{1,0:T(8,128)}) custom-call(f32[16,3,2,32,128]{4,3,2,1,0:T(8,128)} %get-tuple-element.4.bred_hbm, f32[16,128]{1,0:T(8,128)} %get-tuple-element.5.factor_hbm), custom_call_target="tpu_custom_call" | custom-call | tf_op jit(solution)/shard_map/pallas_call | solution.py:450

commit v7 on v6

--- a/solution.py
+++ b/solution.py
@@ -49,8 +49,6 @@
     for peer in greeted[8:]:
         pl.semaphore_signal(barrier, inc=1, device_id=peer, device_id_type=MESH)
 
-    pl.semaphore_wait(barrier, len(greeted))
-
     def y_copies(p, field_ref, st_ref):
         lead = (slice(None),) * (len(field_ref.shape) - 2)
         return [
@@ -66,14 +64,6 @@
 
     def pair_y(p):
         return y_copies(p, perts_hbm.at[pl.ds(2 * p - 2, 2)], st.at[pl.ds(2 * p - 1, 2)])
-
-    for copy in control_y():
-        copy.start()
-
-    @pl.loop(1, 3)
-    def _(p):
-        for copy in pair_y(p):
-            copy.start()
 
     for k in range(members // 4 + 1):
         own_copy(k).wait()
@@ -113,11 +103,16 @@
         ]
 
     everything = [(place, tile) for place in range(3) for tile in (1, 0)]
+    pl.semaphore_wait(barrier, len(greeted))
+
     for key in everything:
         for copy in x_copies(*key):
             copy.start()
 
-    @pl.loop(3, pairs)
+    for copy in control_y():
+        copy.start()
+
+    @pl.loop(1, pairs)
     def _(p):
         for copy in pair_y(p):
             copy.start()
@@ -297,18 +292,20 @@
     for copy in x_copies(1, 0) + x_copies(2, 0):
         copy.wait_recv()
 
-    @pl.loop(1, pairs)
-    def _(p):
-        for copy in pair_y(p):
-            copy.wait_recv()
-        edges([p])
-        bred_out(p).start()
-
-        @pl.when(p % 2 == 0)
-        def _():
-            @pl.loop(0, p // 2)
-            def _(b):
-                products(p // 2 - 1, b, [slice(0, 8), slice(rows - 8, rows)], False)
+    @pl.loop(0, members // 4)
+    def _(q):
+        for p in (2 * q + 1, 2 * q + 2):
+            for copy in pair_y(p):
+                copy.wait_recv()
+        edges([2 * q + 1, 2 * q + 2])
+        for p in (2 * q + 1, 2 * q + 2):
+            bred_out(p).start()
+
+    @pl.loop(0, members // 4)
+    def _(a):
+        @pl.loop(0, a + 1)
+        def _(b):
+            products(a, b, [slice(0, 8), slice(rows - 8, rows)], False)
 
     row_id = lax.broadcasted_iota(jnp.int32, (members, 128), 0)
     col_id = lax.broadcasted_iota(jnp.int32, (members, 128), 1)

time: 39.8 us -> 38.8 us (0.975)
  Pallas kernels: 39.1 us -> 38 us
    pallas_call x1, Pallas kernels: 36.4 us -> 35.3 us  [body(): pl.pallas_call(functools.partial(kernel, nx_dev, ny_dev, members, rows, c...]
where the time goes in v7:
time: 38.8 us; the launch traced here: 38.7 us
  Pallas kernels  38 us (98%)
  between operations  0.64 us (2%)
    pallas_call x1, Pallas kernels, body(): pl.pallas_call(functools.partial(kernel, nx_dev, ny_dev, members, rows, c...  35.3 us
    pallas_call x1, Pallas kernels, body(): pl.pallas_call(functools.partial(apply_kernel, length, members), out_shap...  2.67 us

profile of v7, /device:TPU:1, one launch (start us, length us, event | category | flops | bytes accessed | tf_op | source)
XLA Modules:
  0.0 38.7 jit_solution(18365754456851318005)
XLA Ops:
  0.6 35.3 %shard_map.41 = (f32[16,3,2,32,128]{4,3,2,1,0:T(8,128)}, f32[16,128]{1,0:T(8,128)}) custom-call(f32[3,32,256]{2,1,0:T(8,128)} %ctrl_hbm.1, f32[16,3,32,256]{3,2,1,0:T(8,128)} %perts_hbm.1), custom_call_target="tpu_custom_call" | custom-call | tf_op jit(solution)/shard_map/pallas_call | solution.py:407
  36.0 2.7 %shard_map.42 = (f32[16,3,32,256]{3,2,1,0:T(8,128)}, f32[16,16]{1,0:T(8,128)}) custom-call(f32[16,3,2,32,128]{4,3,2,1,0:T(8,128)} %get-tuple-element.4.bred_hbm, f32[16,128]{1,0:T(8,128)} %get-tuple-element.5.factor_hbm), custom_call_target="tpu_custom_call" | custom-call | tf_op jit(solution)/shard_map/pallas_call | solution.py:447

commit v8 on v7

--- a/solution.py
+++ b/solution.py
@@ -292,7 +292,12 @@
     for copy in x_copies(1, 0) + x_copies(2, 0):
         copy.wait_recv()
 
-    @pl.loop(0, members // 4)
+    def edge_products(a):
+        @pl.loop(0, a + 1)
+        def _(b):
+            products(a, b, [slice(0, 8), slice(rows - 8, rows)], False)
+
+    @pl.loop(0, members // 4 - 1)
     def _(q):
         for p in (2 * q + 1, 2 * q + 2):
             for copy in pair_y(p):
@@ -301,11 +306,18 @@
         for p in (2 * q + 1, 2 * q + 2):
             bred_out(p).start()
 
-    @pl.loop(0, members // 4)
+    @pl.loop(0, members // 4 - 1)
     def _(a):
-        @pl.loop(0, a + 1)
-        def _(b):
-            products(a, b, [slice(0, 8), slice(rows - 8, rows)], False)
+        edge_products(a)
+
+    @pl.loop(pairs - 2, pairs)
+    def _(p):
+        for copy in pair_y(p):
+            copy.wait_recv()
+        edges([p])
+        bred_out(p).start()
+
+    edge_products(members // 4 - 1)
 
     row_id = lax.broadcasted_iota(jnp.int32, (members, 128), 0)
     col_id = lax.broadcasted_iota(jnp.int32, (members, 128), 1)

time: 38.8 us -> 38.9 us (level)
  no operation moved by 1% of the time
where the time goes in v8:
time: 38.9 us; the launch traced here: 38.7 us
  Pallas kernels  38.1 us (98%)
  between operations  0.64 us (2%)
    pallas_call x1, Pallas kernels, body(): pl.pallas_call(functools.partial(kernel, nx_dev, ny_dev, members, rows, c...  35.4 us
    pallas_call x1, Pallas kernels, body(): pl.pallas_call(functools.partial(apply_kernel, length, members), out_shap...  2.67 us

profile of v8, /device:TPU:1, one launch (start us, length us, event | category | flops | bytes accessed | tf_op | source)
XLA Modules:
  0.0 38.7 jit_solution(15152286451372913435)
XLA Ops:
  0.6 35.4 %shard_map.41 = (f32[16,3,2,32,128]{4,3,2,1,0:T(8,128)}, f32[16,128]{1,0:T(8,128)}) custom-call(f32[3,32,256]{2,1,0:T(8,128)} %ctrl_hbm.1, f32[16,3,32,256]{3,2,1,0:T(8,128)} %perts_hbm.1), custom_call_target="tpu_custom_call" | custom-call | tf_op jit(solution)/shard_map/pallas_call | solution.py:419
  36.0 2.7 %shard_map.42 = (f32[16,3,32,256]{3,2,1,0:T(8,128)}, f32[16,16]{1,0:T(8,128)}) custom-call(f32[16,3,2,32,128]{4,3,2,1,0:T(8,128)} %get-tuple-element.4.bred_hbm, f32[16,128]{1,0:T(8,128)} %get-tuple-element.5.factor_hbm), custom_call_target="tpu_custom_call" | custom-call | tf_op jit(solution)/shard_map/pallas_call | solution.py:459

commit v9 on v7

--- a/solution.py
+++ b/solution.py
@@ -49,21 +49,21 @@
     for peer in greeted[8:]:
         pl.semaphore_signal(barrier, inc=1, device_id=peer, device_id_type=MESH)
 
-    def y_copies(p, field_ref, st_ref):
-        lead = (slice(None),) * (len(field_ref.shape) - 2)
+    def y_copies(p, st_ref):
+        lead = (slice(None),) * (len(st_ref.shape) - 2)
         return [
             pltpu.make_async_remote_copy(
-                field_ref.at[lead + (pl.ds(start, HALO),)],
+                st_ref.at[lead + (pl.ds(HALO + start, HALO),)],
                 st_ref.at[lead + (pl.ds(to, HALO),)],
                 y_send.at[way, p], y_recv.at[way, p], device_id=(gx, y_to), device_id_type=MESH)
             for way, (start, to, y_to) in enumerate(((0, HALO + rows, up), (rows - HALO, 0, down)))
         ]
 
     def control_y():
-        return y_copies(0, ctrl_hbm, st.at[0])
+        return y_copies(0, st.at[0])
 
     def pair_y(p):
-        return y_copies(p, perts_hbm.at[pl.ds(2 * p - 2, 2)], st.at[pl.ds(2 * p - 1, 2)])
+        return y_copies(p, st.at[pl.ds(2 * p - 1, 2)])
 
     for k in range(members // 4 + 1):
         own_copy(k).wait()

time: 38.8 us -> 38.8 us (level)
  no operation moved by 1% of the time
where the time goes in v9:
time: 38.8 us; the launch traced here: 38.6 us
  Pallas kernels  38 us (98%)
  between operations  0.64 us (2%)
    pallas_call x1, Pallas kernels, body(): pl.pallas_call(functools.partial(kernel, nx_dev, ny_dev, members, rows, c...  35.3 us
    pallas_call x1, Pallas kernels, body(): pl.pallas_call(functools.partial(apply_kernel, length, members), out_shap...  2.67 us

profile of v9, /device:TPU:1, one launch (start us, length us, event | category | flops | bytes accessed | tf_op | source)
XLA Modules:
  0.0 38.6 jit_solution(15270492229444493667)
XLA Ops:
  0.6 35.3 %shard_map.41 = (f32[16,3,2,32,128]{4,3,2,1,0:T(8,128)}, f32[16,128]{1,0:T(8,128)}) custom-call(f32[3,32,256]{2,1,0:T(8,128)} %ctrl_hbm.1, f32[16,3,32,256]{3,2,1,0:T(8,128)} %perts_hbm.1), custom_call_target="tpu_custom_call" | custom-call | tf_op jit(solution)/shard_map/pallas_call | solution.py:407
  36.0 2.7 %shard_map.42 = (f32[16,3,32,256]{3,2,1,0:T(8,128)}, f32[16,16]{1,0:T(8,128)}) custom-call(f32[16,3,2,32,128]{4,3,2,1,0:T(8,128)} %get-tuple-element.4.bred_hbm, f32[16,128]{1,0:T(8,128)} %get-tuple-element.5.factor_hbm), custom_call_target="tpu_custom_call" | custom-call | tf_op jit(solution)/shard_map/pallas_call | solution.py:447
